TPU v7x, 256 devices: a whole 4x4x8 slice. The times are simulated.
256 devices in a mesh: dp: 4 (over x), expert: 64 (over y, z, core).
Axes of the slice: x: 4, y: 4, z: 8, core: 2. Of those that a mesh axis runs over, the one named last changes fastest.
Arguments:
- tokens: bfloat16 [32768, 4096], P(('dp', 'expert')), may hold values from -6 to 6
- expert_ids: int32 [32768, 2], P(('dp', 'expert')), may hold values from 0 to 63, all different within a row; in each aligned block of 128 rows (0 to 127, 128 to 255, ...) at most 5 rows name the same one
- gate_values: bfloat16 [32768, 2], P(('dp', 'expert')), may hold values from 0.19921875 to 1
- pair_order: int32 [256, 128], P(('dp', 'expert')), may hold values from 0 to 127, each once within a row
- w_gate: bfloat16 [64, 4096, 1536], P('expert', None, 'dp'), may hold values from -0.09375 to 0.09375
- w_up: bfloat16 [64, 4096, 1536], P('expert', None, 'dp'), may hold values from -0.09375 to 0.09375
- w_down: bfloat16 [64, 1536, 4096], P('expert', 'dp'), may hold values from -0.15625 to 0.15625
- sketch: bfloat16 [4096, 256], P('expert'), may hold values from -0.09375 to 0.09375
Outputs:
- mixed: bfloat16 [32768, 4096], P(('dp', 'expert'))
- reading: float32 [4096, 256], P(('dp', 'expert'))
Inputs may be any that keep to these rules, and one draw needn't show every extreme that they name: `expert_ids`: each row names 2 different experts; among the rows of one device no expert is named more than 5 times, a bound that some block reaches. `pair_order`: each row is a permutation of 0 .. 127, given as row numbers inside its device's block; entries 2 p and 2 p + 1 are the positive and the negative token of pair p.
All inputs are finite; a program needn't handle non-finite values.
Results may differ from a plain program's by a relative error of at most 0.022.
Values may be sent and summed in bfloat16 or wider, within the bound.
No kernel may reach another device: no remote copies, remote signals or barrier semaphores. Data moves between devices by JAX's collectives and lax.ppermute only.
A program may use at most 128 MiB of HBM per device.

v0:
```python
import math

import jax
import jax.numpy as jnp
from jax import lax
from jax.sharding import PartitionSpec as P


def route_slots(picks_ids, experts, capacity):
    flat_ids = picks_ids.reshape(-1)
    onehot = (flat_ids[:, None] == jnp.arange(experts, dtype=jnp.int32)[None, :]).astype(jnp.int32)
    slot_rank = jnp.sum((jnp.cumsum(onehot, axis=0) - onehot) * onehot, axis=1)
    return flat_ids * capacity + slot_rank


def dispatch_rows(token_rows, slot_index, experts, capacity):
    rows_dev, width = token_rows.shape
    slot_grid = slot_index.reshape(rows_dev, -1)
    select = jnp.any(
        slot_grid[None, :, :] == jnp.arange(experts * capacity, dtype=jnp.int32)[:, None, None],
        axis=2,
    )
    placed = jnp.dot(select.astype(jnp.bfloat16), token_rows, preferred_element_type=jnp.float32)
    return placed.astype(jnp.bfloat16).reshape(experts, capacity, width)


def shards(tokens, expert_ids, gate_values, pair_order, w_gate, w_up, w_down, sketch):
    rows_dev, width = tokens.shape
    chosen = expert_ids.shape[1]
    experts = lax.axis_size("expert")
    groups = lax.axis_size("dp")
    capacity = max(2, 5 * rows_dev * chosen // (4 * experts))
    slot_index = route_slots(expert_ids, experts, capacity)
    gate_proj = w_gate[0]
    up_proj = w_up[0]
    down_proj = w_down[0]
    outgoing = dispatch_rows(tokens, slot_index, experts, capacity)
    arrived = lax.all_to_all(outgoing, "expert", split_axis=0, concat_axis=0, tiled=True)
    gathered = lax.all_gather(arrived, "dp", axis=0, tiled=True)
    picked = gathered.reshape(experts * lax.axis_size("dp") * capacity, width)
    gate_act = jnp.dot(picked, gate_proj, preferred_element_type=jnp.float32)
    up_act = jnp.dot(picked, up_proj, preferred_element_type=jnp.float32)
    activation = (jax.nn.silu(gate_act) * up_act).astype(jnp.bfloat16)
    summed = lax.psum_scatter(
        jnp.dot(activation, down_proj, preferred_element_type=jnp.float32)
        .reshape(experts * lax.axis_size("dp"), capacity, width)
        .astype(jnp.bfloat16),
        "dp",
        scatter_dimension=0,
        tiled=True,
    )
    returned = lax.all_to_all(summed, "expert", split_axis=0, concat_axis=0, tiled=True)
    slot_grid = slot_index.reshape(rows_dev, chosen)
    matches = (
        slot_grid[:, :, None] == jnp.arange(experts * capacity, dtype=jnp.int32)[None, None, :]
    )
    weights = jnp.sum(
        jnp.where(matches, gate_values[:, :, None], jnp.zeros((), jnp.bfloat16)), axis=1
    )
    mixed = jnp.dot(
        weights, returned.reshape(experts * capacity, width), preferred_element_type=jnp.float32
    ).astype(jnp.bfloat16)
    pair_rows = pair_order[0]
    positive = jnp.take(mixed, pair_rows[0::2], axis=0).astype(jnp.float32)
    negative = jnp.take(mixed, pair_rows[1::2], axis=0).astype(jnp.float32)
    contrast = (positive - negative).astype(jnp.bfloat16)
    projected = jnp.dot(
        contrast,
        lax.all_gather(sketch, "expert", axis=0, tiled=True),
        preferred_element_type=jnp.float32,
    ).astype(jnp.bfloat16)
    covariance = lax.dot_general(
        contrast, projected, (((0,), (0,)), ((), ())), preferred_element_type=jnp.float32
    )
    reading = lax.psum_scatter(covariance, ("dp", "expert"), scatter_dimension=0, tiled=True)
    pairs_all = rows_dev // 2 * groups * experts
    reading = reading * (1.0 / math.sqrt(pairs_all))
    return (mixed, reading)


def solution(mesh):
    return jax.shard_map(
        shards,
        mesh=mesh,
        in_specs=(
            P(("dp", "expert"), None),
            P(("dp", "expert"), None),
            P(("dp", "expert"), None),
            P(("dp", "expert"), None),
            P("expert", None, "dp"),
            P("expert", None, "dp"),
            P("expert", "dp", None),
            P("expert", None),
        ),
        out_specs=(P(("dp", "expert"), None), P(("dp", "expert"), None)),
        check_vma=False,
    )
```

profile of v0, /device:TPU:1, one launch (start us, length us, event | category | flops | bytes accessed | tf_op | source)
XLA Modules:
  0.0 1805.3 jit_solution(13525741573780310119)
XLA Ops:
  8.0 0.0 copy-start
  8.0 0.0 all-gather.3.cloned.1.call-start
  8.1 0.9 copy.43
  9.0 0.1 eq.55
  9.1 0.1 eq.51
  9.3 0.6 reduce-window.6
  9.9 0.2 slice_reduce_fusion
  10.1 0.1 fusion.24
  10.2 0.1 reduce_sum.24
  10.4 0.1 copy.46
  10.5 0.7 multiply_add_fusion
  11.2 3.6 convolution_convert_fusion.1
  14.8 4.7 reshape.52
  19.5 109.3 %all_to_all.10 = bf16[64,5,4096]{2,1,0:T(8,128)(2,1)S(1)} all-to-all(bf16[64,5,4096]{2,1,0:T(8,128)(2,1)} %reshape.52), channel_id=1, replica_groups=mesh['dp'=4,'expert'=64] {'expert'}, dimensions={0} | all-to-all | bytes 5242880 | tf_op jit(solution)/shard_map/all_to_all | solution.py:38
  128.8 3.2 copy.47
  132.1 0.0 all-gather.3.cloned.1.call-update
  132.1 0.2 reduce-scatter.3.cloned.1.call-start
  132.3 99.7 %all-gather.3.cloned.1.call-done = bf16[256,5,4096]{2,0,1:T(8,128)(2,1)} async-done(((bf16[64,5,4096]{2,0,1:T(8,128)(2,1)}), bf16[256,5,4096]{2,0,1:T(8,128)(2,1)}) %all-gather.3.cloned.1.call-update) | async-done | bytes 10485776 | tf_op jit(solution)/shard_map/all_gather | solution.py:39
  232.1 15.2 copy.48
  247.3 16.8 reshape.53
  264.1 0.0 copy-start.1
  264.1 9.3 fusion.2
  273.5 0.0 copy-done.1
  273.5 0.0 copy-done.3
  273.5 6.9 fusion.4
  280.4 3.0 dot_general.26
  283.4 0.0 copy-done
  283.4 9.6 convolution_convert_fusion
  293.0 0.0 reduce-scatter.3.cloned.1.call-update
  293.0 101.3 %reduce-scatter.3.cloned.1.call-done = bf16[64,5,4096]{2,0,1:T(8,128)(2,1)} async-done(((bf16[256,5,4096]{2,0,1:T(8,128)(2,1)}), bf16[64,5,4096]{2,0,1:T(8,128)(2,1)}) %reduce-scatter.3.cloned.1.call-update) | async-done | bytes 2621456 | tf_op jit(solution)/shard_map/reduce_scatter | solution.py:44
  394.2 5.2 copy.50
  399.5 11.0 all-to-all-start.1
  410.4 0.0 all-gather.5.cloned.1.call-start
  410.5 0.5 all-gather.5.cloned.1.call-update
  411.0 0.0 reduce-scatter.5.cloned.1.call-start
  411.1 0.0 copy-done.4
  411.1 0.2 slice.14
  411.2 0.2 slice.15
  411.4 0.0 copy-done.2
  411.5 101.0 %all-to-all-done.1 = bf16[64,5,4096]{2,1,0:T(8,128)(2,1)} async-done(((bf16[64,5,4096]{2,1,0:T(8,128)(2,1)}), bf16[64,5,4096]{2,1,0:T(8,128)(2,1)}, u32[]{:S(2)}, u32[]{:S(2)}) %all-to-all-start.1) | async-done | bytes 2621472 | tf_op jit(solution)/shard_map/all_to_all | solution.py:52
  512.5 4.8 reshape.54
  517.2 3.5 convolution_convert_fusion.2
  520.7 3.5 gather_fusion
  524.2 3.5 gather_fusion.1
  527.8 6.0 fusion.7
  533.7 0.0 reduce-scatter.5.cloned.1.call-update
  533.8 1262.8 %reduce-scatter.5.cloned.1.call-done = f32[16,256]{1,0:T(8,128)} async-done(((f32[4096,256]{1,0:T(8,128)}), f32[16,256]{1,0:T(8,128)}) %reduce-scatter.5.cloned.1.call-update) | async-done | bytes 16400 | tf_op jit(solution)/shard_map/reduce_scatter | solution.py:75
  1796.5 1.3 broadcast_multiply_fusion
  (14 shorter events, 0.2 us)
Async XLA Ops:
  8.0 275.4 %copy-start = (bf16[1,384,4096]{2,1,0:T(8,128)(2,1)S(1)}, bf16[1,384,4096]{2,1,0:T(8,128)(2,1)}, u32[]{:S(2)}) copy-start(bf16[1,384,4096]{2,1,0:T(8,128)(2,1)} %param.16) | copy-start | bytes 9437188
  8.0 224.1 %all-gather.3.cloned.1.call-start = ((), (), s32[]{:S(2)}) async-start(), calls=%async_computation.4 | async-start | bytes 13107200 | tf_op jit(solution)/shard_map/all_gather | solution.py:39
  132.1 262.2 %reduce-scatter.3.cloned.1.call-start = ((), (), s32[]{:S(2)}) async-start(), calls=%async_computation.5 | async-start | bytes 13107200 | tf_op jit(solution)/shard_map/reduce_scatter | solution.py:44
  264.1 9.4 copy-start.1
  264.1 9.4 copy-start.3
  399.5 11.6 copy-start.4
  399.5 12.0 copy-start.2
  399.5 113.0 %all-to-all-start.1 = ((bf16[64,5,4096]{2,1,0:T(8,128)(2,1)}), bf16[64,5,4096]{2,1,0:T(8,128)(2,1)}, u32[]{:S(2)}, u32[]{:S(2)}) async-start(bf16[64,5,4096]{2,1,0:T(8,128)(2,1)} %copy.50), calls=%async_computation.2 | async-start | bytes 8388608 | tf_op jit(solution)/shard_map/all_to_all | solution.py:52
  410.4 117.3 %all-gather.5.cloned.1.call-start = ((), (), s32[]{:S(2)}) async-start(), calls=%async_computation.6 | async-start | bytes 2129920 | tf_op jit(solution)/shard_map/all_gather | solution.py:69
  411.0 1385.5 %reduce-scatter.5.cloned.1.call-start = ((), (), s32[]{:S(2)}) async-start(), calls=%async_computation.7 | async-start | bytes 4210688 | tf_op jit(solution)/shard_map/reduce_scatter | solution.py:75
Sparse Core Ops, SparseCore 0:
  132.2 99.8 all-gather.2
  293.1 101.0 reduce-scatter.2
Sparse Core Ops, SparseCore 1:
  413.7 93.8 all-gather.4
  533.9 1262.6 reduce-scatter.4
where the time goes:
time: 1810 us
  waiting for transfers between devices  1570 us (87%)
  blocking collectives  109 us (6%)
  local copies, waits for them, and re-layouts  62 us (3%)
  matrix products  38.9 us (2%)
    reduce_scatter x1, waiting for transfers between devices, shards(): lax.psum_scatter(covariance, ('dp', 'expert'), scatter_dimension=0, tiled...  1260 us
    all_to_all x1, blocking collectives, shards(): lax.all_to_all(outgoing, 'expert', split_axis=0, concat_axis=0, tiled=True)  109 us
    reduce_scatter x1, waiting for transfers between devices, shards(): lax.psum_scatter(jnp.dot(activation, down_proj, preferred_element_type=jn...  101 us
    all_to_all x1, waiting for transfers between devices, shards(): lax.all_to_all(summed, 'expert', split_axis=0, concat_axis=0, tiled=True)  101 us
    all_gather x1, waiting for transfers between devices, shards(): gathered = lax.all_gather(arrived, 'dp', axis=0, tiled=True)  99.7 us
  transfers between devices with their start and end apart: 5, of which 4 were waited for; matrix products, arithmetic and copies ran while one was open for 1% of the time, Pallas kernels for 0%

commit v1 on v0

v1 whole, which is shorter than its diff:
```python
import math

import jax
import jax.numpy as jnp
from jax import lax
from jax.sharding import PartitionSpec as P

CHUNKS = (1, 2, 2)


def pick_ranks(ids):
    rows = ids.shape[0]
    earlier = jnp.arange(rows)[None, :] < jnp.arange(rows)[:, None]
    same = ids[:, :, None, None] == ids[None, None, :, :]
    return jnp.sum((same & earlier[:, None, :, None]).astype(jnp.int32), axis=(2, 3))


def shards(tokens, expert_ids, gate_values, pair_order, w_gate, w_up, w_down, sketch):
    rows_dev, width = tokens.shape
    experts = lax.axis_size("expert")
    groups = lax.axis_size("dp")
    lanes = 128
    tall = width // lanes
    gate_proj, up_proj, down_proj = w_gate[0], w_up[0], w_down[0]
    ranks = pick_ranks(expert_ids)

    def place_of(first, count):
        inside = (ranks >= first) & (ranks < first + count)
        return jnp.where(inside, expert_ids * count + ranks - first, -1)

    places, first = [], 0
    for count in CHUNKS:
        places.append(place_of(first, count))
        first += count

    full_sketch = lax.all_gather(sketch, "expert", axis=0, tiled=True)

    arrived = []
    for count, place in zip(CHUNKS, places):
        spots = jnp.arange(experts * count, dtype=jnp.int32)
        select = jnp.any(place[None, :, :] == spots[:, None, None], axis=2)
        placed = jnp.dot(select.astype(jnp.bfloat16), tokens, preferred_element_type=jnp.float32)
        outgoing = placed.astype(jnp.bfloat16).reshape(experts, count * tall, lanes)
        incoming = lax.all_to_all(outgoing, "expert", split_axis=0, concat_axis=0, tiled=True)
        arrived.append(incoming.reshape(experts * count, width))

    mixed_sum = jnp.zeros((rows_dev, width), jnp.float32)
    for count, place, rows in zip(CHUNKS, places, arrived):
        picked = lax.all_gather(rows, "dp", axis=0, tiled=True)
        gate_act = jnp.dot(picked, gate_proj, preferred_element_type=jnp.float32)
        up_act = jnp.dot(picked, up_proj, preferred_element_type=jnp.float32)
        activation = (jax.nn.silu(gate_act) * up_act).astype(jnp.bfloat16)
        partial = jnp.dot(activation, down_proj, preferred_element_type=jnp.float32)
        summed = lax.psum_scatter(
            partial.astype(jnp.bfloat16), "dp", scatter_dimension=0, tiled=True
        )
        summed = summed.reshape(experts, count * tall, lanes)
        returned = lax.all_to_all(summed, "expert", split_axis=0, concat_axis=0, tiled=True)
        returned = returned.reshape(experts * count, width)
        spots = jnp.arange(experts * count, dtype=jnp.int32)
        matches = place[:, :, None] == spots[None, None, :]
        weights = jnp.sum(
            jnp.where(matches, gate_values[:, :, None], jnp.zeros((), jnp.bfloat16)), axis=1
        )
        mixed_sum = mixed_sum + jnp.dot(weights, returned, preferred_element_type=jnp.float32)
    mixed = mixed_sum.astype(jnp.bfloat16)

    pairs = rows_dev // 2
    order = pair_order[0].reshape(pairs, 2)
    row_ids = jnp.arange(rows_dev, dtype=jnp.int32)
    signs = (order[:, 0:1] == row_ids[None, :]).astype(jnp.bfloat16) - (
        order[:, 1:2] == row_ids[None, :]
    ).astype(jnp.bfloat16)
    contrast = jnp.dot(signs, mixed, preferred_element_type=jnp.float32).astype(jnp.bfloat16)
    projected = jnp.dot(contrast, full_sketch, preferred_element_type=jnp.float32)
    projected = lax.all_gather(projected.astype(jnp.bfloat16), "dp", axis=0, tiled=True)
    columns = jnp.transpose(contrast.reshape(pairs, groups, width // groups), (1, 0, 2))
    columns = lax.all_to_all(columns, "dp", split_axis=0, concat_axis=0, tiled=True)
    columns = columns.reshape(groups * pairs, width // groups)
    covariance = lax.dot_general(
        columns, projected, (((0,), (0,)), ((), ())), preferred_element_type=jnp.float32
    )
    parts = covariance.astype(jnp.bfloat16).reshape(experts, -1, covariance.shape[1])
    parts = lax.all_to_all(parts, "expert", split_axis=0, concat_axis=0, tiled=True)
    reading = jnp.sum(parts.astype(jnp.float32), axis=0)
    reading = reading * (1.0 / math.sqrt(pairs * groups * experts))
    return (mixed, reading)


def solution(mesh):
    return jax.shard_map(
        shards,
        mesh=mesh,
        in_specs=(
            P(("dp", "expert"), None),
            P(("dp", "expert"), None),
            P(("dp", "expert"), None),
            P(("dp", "expert"), None),
            P("expert", None, "dp"),
            P("expert", None, "dp"),
            P("expert", "dp", None),
            P("expert", None),
        ),
        out_specs=(P(("dp", "expert"), None), P(("dp", "expert"), None)),
        check_vma=False,
    )
```

time: 1810 us -> 433 us (0.24)
  waiting for transfers between devices: 1570 us -> 153 us
  local copies, waits for them, and re-layouts: 62 us -> 24.2 us
  blocking collectives: 109 us -> 138 us
  starting transfers between devices: 11.3 us -> 37.4 us
  matrix products: 38.9 us -> 60.3 us
    reduce_scatter x2 -> x3, waiting for transfers between devices: 1360 us -> 95.5 us  [shards(): lax.psum_scatter(partial.astype(jnp.bfloat16), 'dp', scatter_dimension=0,...]
    all_to_all x1 -> x3, waiting for transfers between devices: 101 us -> 26.4 us  [shards(): lax.all_to_all(summed, 'expert', split_axis=0, concat_axis=0, tiled=True)]
    all_gather x2 -> x4, waiting for transfers between devices: 99.7 us -> 30.5 us  [the longest x3 30.4 us: shards(): picked = lax.all_gather(rows, 'dp', axis=0, tiled=True)]
    all_to_all x0 -> x1, blocking collectives: none -> 26.8 us  [shards(): lax.all_to_all(parts, 'expert', split_axis=0, concat_axis=0, tiled=True)]
    all_to_all x1 -> x3, starting transfers between devices: 11 us -> 32.8 us  [shards(): lax.all_to_all(summed, 'expert', split_axis=0, concat_axis=0, tiled=True)]
    dot_general x5 -> x12, matrix products: 29.5 us -> 43 us  [the longest x3 26.5 us: shards(): partial = jnp.dot(activation, down_proj, preferred_element_type=jnp.float32)]
    all_to_all x1 -> x3, blocking collectives: 109 us -> 100 us  [shards(): lax.all_to_all(outgoing, 'expert', split_axis=0, concat_axis=0, tiled=True)]
  transfers between devices with their start and end apart: 5 -> 11, of which waited for: 4 -> 5; matrix products, arithmetic and copies ran while one was open for 1% -> 19% of each run, Pallas kernels for 0% -> 0%
where the time goes in v1:
time: 433 us; the launch traced here: 432 us
  waiting for transfers between devices  153 us (35%)
  blocking collectives  138 us (32%)
  matrix products  60.3 us (14%)
  starting transfers between devices  37.4 us (9%)
  local copies, waits for them, and re-layouts  24.2 us (6%)
  between operations  15.8 us (4%)
    all_to_all x3, blocking collectives, shards(): lax.all_to_all(outgoing, 'expert', split_axis=0, concat_axis=0, tiled=True)  100 us
    reduce_scatter x3, waiting for transfers between devices, shards(): lax.psum_scatter(partial.astype(jnp.bfloat16), 'dp', scatter_dimension=0,...  95.5 us
    all_to_all x3, starting transfers between devices, shards(): lax.all_to_all(summed, 'expert', split_axis=0, concat_axis=0, tiled=True)  32.8 us
    all_gather x3, waiting for transfers between devices, shards(): picked = lax.all_gather(rows, 'dp', axis=0, tiled=True)  30.4 us
    all_to_all x1, blocking collectives, shards(): lax.all_to_all(parts, 'expert', split_axis=0, concat_axis=0, tiled=True)  26.8 us
    dot_general x3, matrix products, shards(): partial = jnp.dot(activation, down_proj, preferred_element_type=jnp.float32)  26.5 us
    all_to_all x3, waiting for transfers between devices, shards(): lax.all_to_all(summed, 'expert', split_axis=0, concat_axis=0, tiled=True)  26.4 us
    dot_general x3, matrix products, shards(): gate_act = jnp.dot(picked, gate_proj, preferred_element_type=jnp.float32)  17.3 us
  transfers between devices with their start and end apart: 11, of which 5 were waited for; matrix products, arithmetic and copies ran while one was open for 19% of the time, Pallas kernels for 0%

profile of v1, /device:TPU:1, one launch (start us, length us, event | category | flops | bytes accessed | tf_op | source)
XLA Modules:
  0.0 431.8 jit_solution(12024456891787104285)
XLA Ops:
  8.1 1.0 convert_reduce_fusion.1
  9.1 0.7 and_select_fusion.1
  9.8 1.5 fusion.28
  11.4 30.3 %all_to_all.40 = bf16[64,32,128]{2,1,0:T(8,128)(2,1)S(1)} all-to-all(bf16[64,32,128]{2,1,0:T(8,128)(2,1)S(1)} %bitcast.88), channel_id=1, replica_groups=mesh['dp'=4,'expert'=64] {'expert'}, dimensions={0} | all-to-all | bytes 1048576 | tf_op jit(solution)/shard_map/all_to_all | solution.py:44
  41.7 1.0 copy.43
  42.9 2.6 convolution_convert_fusion.4
  45.5 2.3 reshape.74
  47.8 34.9 %all_to_all.41 = bf16[64,64,128]{2,1,0:T(8,128)(2,1)} all-to-all(bf16[64,64,128]{2,1,0:T(8,128)(2,1)} %reshape.74), channel_id=1, replica_groups=mesh['dp'=4,'expert'=64] {'expert'}, dimensions={0} | all-to-all | bytes 2097152 | tf_op jit(solution)/shard_map/all_to_all | solution.py:44
  82.8 2.3 reshape.75
  85.2 2.7 convolution_convert_fusion.3
  87.8 2.4 reshape.78
  90.2 34.9 %all_to_all.42 = bf16[64,64,128]{2,1,0:T(8,128)(2,1)} all-to-all(bf16[64,64,128]{2,1,0:T(8,128)(2,1)} %reshape.78), channel_id=1, replica_groups=mesh['dp'=4,'expert'=64] {'expert'}, dimensions={0} | all-to-all | bytes 2097152 | tf_op jit(solution)/shard_map/all_to_all | solution.py:44
  125.0 2.3 reshape.79
  127.4 4.5 %fusion.14 = f32[256,384]{1,0:T(8,128)} fusion(bf16[256,4096]{1,0:T(8,128)(2,1)} %all-gather.5.cloned.1.call-done, bf16[1,4096,384]{2,1,0:T(8,128)(2,1)} %param.12), kind=kOutput, calls=%fused_computation.23 | convolution fusion | flops 805306368 | bytes 5636096 | tf_op jit(solution)/shard_map/dot_general | solution.py:50
  132.0 6.4 %convolution_convert_fusion.2 = bf16[256,4096]{1,0:T(8,128)(2,1)} fusion(bf16[1,384,4096]{2,1,0:T(8,128)(2,1)S(1)} %copy-done, bf16[256,4096]{1,0:T(8,128)(2,1)} %all-gather.5.cloned.1.call-done, bf16[1,4096,384]{2,1,0:T(8,128)(2,1)} %param.13, f32[256,384]{1,0:T(8,128)} %fusion.14), kind=kOutput, calls=%fused_computation.2 | convolution fusion | flops 1612251136 | bytes 10878976 | tf_op jit(solution)/shard_map/dot_general | solution.py:53
  138.4 0.2 reduce-scatter.6.cloned.1.call-start
  138.7 6.4 %fusion.12 = f32[512,384]{1,0:T(8,128)} fusion(bf16[512,4096]{1,0:T(8,128)(2,1)} %all-gather.7.cloned.1.call-done, bf16[1,4096,384]{2,1,0:T(8,128)(2,1)} %param.12), kind=kOutput, calls=%fused_computation.21 | convolution fusion | flops 1610612736 | bytes 8126464 | tf_op jit(solution)/shard_map/dot_general | solution.py:50
  145.0 10.4 %convolution_convert_fusion.1 = bf16[512,4096]{1,0:T(8,128)(2,1)} fusion(bf16[1,384,4096]{2,1,0:T(8,128)(2,1)S(1)} %copy-done, bf16[512,4096]{1,0:T(8,128)(2,1)} %all-gather.7.cloned.1.call-done, bf16[1,4096,384]{2,1,0:T(8,128)(2,1)} %param.13, f32[512,384]{1,0:T(8,128)} %fusion.12), kind=kOutput, calls=%fused_computation.1 | convolution fusion | flops 3224502272 | bytes 15466496 | tf_op jit(solution)/shard_map/dot_general | solution.py:53
  155.5 30.4 %all-gather.9.cloned.1.call-done = bf16[512,4096]{1,0:T(8,128)(2,1)} async-done(((bf16[128,4096]{1,0:T(8,128)(2,1)}), bf16[512,4096]{1,0:T(8,128)(2,1)}) %all-gather.9.cloned.1.call-update) | async-done | bytes 4194320 | tf_op jit(solution)/shard_map/all_gather | solution.py:49
  185.9 6.4 %fusion.10 = f32[512,384]{1,0:T(8,128)} fusion(bf16[512,4096]{1,0:T(8,128)(2,1)} %all-gather.9.cloned.1.call-done, bf16[1,4096,384]{2,1,0:T(8,128)(2,1)} %param.12), kind=kOutput, calls=%fused_computation.19 | convolution fusion | flops 1610612736 | bytes 8126464 | tf_op jit(solution)/shard_map/dot_general | solution.py:50
  192.3 9.7 %convolution_convert_fusion = bf16[512,4096]{1,0:T(8,128)(2,1)} fusion(bf16[1,384,4096]{2,1,0:T(8,128)(2,1)S(1)} %copy-done, bf16[512,4096]{1,0:T(8,128)(2,1)} %all-gather.9.cloned.1.call-done, bf16[1,4096,384]{2,1,0:T(8,128)(2,1)} %param.13, f32[512,384]{1,0:T(8,128)} %fusion.10), kind=kOutput, calls=%fused_computation | convolution fusion | flops 3224502272 | bytes 15466496 | tf_op jit(solution)/shard_map/dot_general | solution.py:53
  202.0 18.9 %reduce-scatter.4.cloned.1.call-done = bf16[64,4096]{1,0:T(8,128)(2,1)} async-done(((bf16[256,4096]{1,0:T(8,128)(2,1)}), bf16[64,4096]{1,0:T(8,128)(2,1)}) %reduce-scatter.4.cloned.1.call-update) | async-done | bytes 524304 | tf_op jit(solution)/shard_map/reduce_scatter | solution.py:54
  221.0 1.9 copy.35
  222.9 10.8 %all-to-all-start.1 = ((bf16[64,32,128]{2,1,0:T(8,128)(2,1)}), bf16[64,32,128]{2,1,0:T(8,128)(2,1)}, u32[]{:S(2)}, u32[]{:S(2)}) async-start(bf16[64,32,128]{2,1,0:T(8,128)(2,1)} %bitcast.86), calls=%async_computation.2 | async-start | bytes 1048576 | tf_op jit(solution)/shard_map/all_to_all | solution.py:58
  233.7 39.0 %reduce-scatter.6.cloned.1.call-done = bf16[128,4096]{1,0:T(8,128)(2,1)} async-done(((bf16[512,4096]{1,0:T(8,128)(2,1)}), bf16[128,4096]{1,0:T(8,128)(2,1)}) %reduce-scatter.6.cloned.1.call-update) | async-done | bytes 1048592 | tf_op jit(solution)/shard_map/reduce_scatter | solution.py:54
  272.7 2.3 reshape.76
  275.0 11.0 %all-to-all-start.3 = ((bf16[64,64,128]{2,1,0:T(8,128)(2,1)}), bf16[64,64,128]{2,1,0:T(8,128)(2,1)}, u32[]{:S(2)}, u32[]{:S(2)}) async-start(bf16[64,64,128]{2,1,0:T(8,128)(2,1)} %reshape.76), calls=%async_computation.5 | async-start | bytes 2097152 | tf_op jit(solution)/shard_map/all_to_all | solution.py:58
  286.0 0.5 all-gather.11.cloned.1.call-update
  286.6 37.6 %reduce-scatter.8.cloned.1.call-done = bf16[128,4096]{1,0:T(8,128)(2,1)} async-done(((bf16[512,4096]{1,0:T(8,128)(2,1)}), bf16[128,4096]{1,0:T(8,128)(2,1)}) %reduce-scatter.8.cloned.1.call-update) | async-done | bytes 1048592 | tf_op jit(solution)/shard_map/reduce_scatter | solution.py:54
  324.2 2.3 reshape.80
  326.6 11.0 %all-to-all-start.5 = ((bf16[64,64,128]{2,1,0:T(8,128)(2,1)}), bf16[64,64,128]{2,1,0:T(8,128)(2,1)}, u32[]{:S(2)}, u32[]{:S(2)}) async-start(bf16[64,64,128]{2,1,0:T(8,128)(2,1)} %reshape.80), calls=%async_computation.8 | async-start | bytes 2097152 | tf_op jit(solution)/shard_map/all_to_all | solution.py:58
  337.6 0.5 broadcast.48
  338.1 0.7 reduce.10
  339.3 2.9 fusion.41
  342.2 2.3 reshape.77
  344.5 26.4 %all-to-all-done.5 = bf16[64,64,128]{2,1,0:T(8,128)(2,1)} async-done(((bf16[64,64,128]{2,1,0:T(8,128)(2,1)}), bf16[64,64,128]{2,1,0:T(8,128)(2,1)}, u32[]{:S(2)}, u32[]{:S(2)}) %all-to-all-start.5) | async-done | bytes 1048608 | tf_op jit(solution)/shard_map/all_to_all | solution.py:58
  370.9 2.3 reshape.81
  373.2 2.4 convolution_add_fusion.1
  375.6 0.4 fusion
  376.1 0.3 convolution_convert_fusion.5
  376.5 0.8 copy-done.1
  377.3 0.8 copy.44
  378.1 4.1 all-to-all-start.6
  382.3 2.2 convolution_convert_fusion.8
  384.5 10.9 %all_gather.19 = bf16[256,256]{1,0:T(8,128)(2,1)S(1)} all-gather(bf16[64,256]{1,0:T(8,128)(2,1)S(1)} %convolution_convert_fusion.8), channel_id=1, replica_groups=mesh['dp'=4,'expert'=64] {'dp'}, dimensions={0}, use_global_device_ids=true | all-gather | bytes 163840 | tf_op jit(solution)/shard_map/all_gather | solution.py:76
  395.5 1.4 convolution_convert_fusion.7
  396.9 26.8 %all_to_all.43 = bf16[64,16,256]{2,1,0:T(8,128)(2,1)S(1)} all-to-all(bf16[64,16,256]{2,1,0:T(8,128)(2,1)S(1)} %bitcast.87), channel_id=1, replica_groups=mesh['dp'=4,'expert'=64] {'expert'}, dimensions={0} | all-to-all | bytes 1048576 | tf_op jit(solution)/shard_map/all_to_all | solution.py:84
  423.7 0.6 broadcast_multiply_fusion
  (38 shorter events, 1.2 us)
Async XLA Ops:
  8.0 124.0 %copy-start = (bf16[1,384,4096]{2,1,0:T(8,128)(2,1)S(1)}, bf16[1,384,4096]{2,1,0:T(8,128)(2,1)}, u32[]{:S(2)}) copy-start(bf16[1,384,4096]{2,1,0:T(8,128)(2,1)} %param.14) | copy-start | bytes 9437188
  8.0 119.4 %all-gather.5.cloned.1.call-start = ((), (), s32[]{:S(2)}) async-start(), calls=%async_computation.11 | async-start | bytes 2621440 | tf_op jit(solution)/shard_map/all_gather | solution.py:49
  42.8 95.9 %all-gather.7.cloned.1.call-start = ((), (), s32[]{:S(2)}) async-start(), calls=%async_computation.13 | async-start | bytes 5242880 | tf_op jit(solution)/shard_map/all_gather | solution.py:49
  85.1 100.8 %all-gather.9.cloned.1.call-start = ((), (), s32[]{:S(2)}) async-start(), calls=%async_computation.15 | async-start | bytes 5242880 | tf_op jit(solution)/shard_map/all_gather | solution.py:49
  127.4 93.6 %reduce-scatter.4.cloned.1.call-start = ((), (), s32[]{:S(2)}) async-start(), calls=%async_computation.12 | async-start | bytes 2621440 | tf_op jit(solution)/shard_map/reduce_scatter | solution.py:54
  138.4 134.3 %reduce-scatter.6.cloned.1.call-start = ((), (), s32[]{:S(2)}) async-start(), calls=%async_computation.14 | async-start | bytes 5242880 | tf_op jit(solution)/shard_map/reduce_scatter | solution.py:54
  155.5 168.8 %reduce-scatter.8.cloned.1.call-start = ((), (), s32[]{:S(2)}) async-start(), calls=%async_computation.16 | async-start | bytes 5242880 | tf_op jit(solution)/shard_map/reduce_scatter | solution.py:54
  222.9 52.1 %all-to-all-start.1 = ((bf16[64,32,128]{2,1,0:T(8,128)(2,1)}), bf16[64,32,128]{2,1,0:T(8,128)(2,1)}, u32[]{:S(2)}, u32[]{:S(2)}) async-start(bf16[64,32,128]{2,1,0:T(8,128)(2,1)} %bitcast.86), calls=%async_computation.2 | async-start | bytes 1048576 | tf_op jit(solution)/shard_map/all_to_all | solution.py:58
  275.0 63.1 %copy-start.5 = (s32[1,128]{1,0:T(1,128)S(1)}, s32[1,128]{1,0:T(1,128)}, u32[]{:S(2)}) copy-start(s32[1,128]{1,0:T(1,128)} %param.11) | copy-start | bytes 1540
  275.0 64.1 %copy-start.4 = (bf16[128,2]{0,1:T(2,128)(2,1)S(1)}, bf16[128,2]{0,1:T(2,128)(2,1)}, u32[]{:S(2)}) copy-start(bf16[128,2]{0,1:T(2,128)(2,1)} %param.10) | copy-start | bytes 1540
  275.0 51.6 %all-to-all-start.3 = ((bf16[64,64,128]{2,1,0:T(8,128)(2,1)}), bf16[64,64,128]{2,1,0:T(8,128)(2,1)}, u32[]{:S(2)}, u32[]{:S(2)}) async-start(bf16[64,64,128]{2,1,0:T(8,128)(2,1)} %reshape.76), calls=%async_computation.5 | async-start | bytes 2097152 | tf_op jit(solution)/shard_map/all_to_all | solution.py:58
  286.0 96.3 %all-gather.11.cloned.1.call-start = ((), (), s32[]{:S(2)}) async-start(), calls=%async_computation.17 | async-start | bytes 2129920 | tf_op jit(solution)/shard_map/all_gather | solution.py:36
  326.6 44.3 %all-to-all-start.5 = ((bf16[64,64,128]{2,1,0:T(8,128)(2,1)}), bf16[64,64,128]{2,1,0:T(8,128)(2,1)}, u32[]{:S(2)}, u32[]{:S(2)}) async-start(bf16[64,64,128]{2,1,0:T(8,128)(2,1)} %reshape.80), calls=%async_computation.8 | async-start | bytes 2097152 | tf_op jit(solution)/shard_map/all_to_all | solution.py:58
  373.2 2.4 copy-start.3
  376.1 2.0 copy-start.2
  376.4 0.8 copy-start.1
  378.1 17.3 %all-to-all-start.6 = ((bf16[4,64,1024]{2,1,0:T(8,128)(2,1)}), bf16[4,64,1024]{2,1,0:T(8,128)(2,1)}, u32[]{:S(2)}, u32[]{:S(2)}) async-start(bf16[4,64,1024]{2,1,0:T(8,128)(2,1)} %bitcast.85), calls=%async_computation.9 | async-start | bytes 1048576 | tf_op jit(solution)/shard_map/all_to_all | solution.py:78
Sparse Core Ops, SparseCore 0:
  42.9 30.2 all-gather.4
  85.2 47.6 all-gather.6
  134.7 51.1 all-gather.8
  188.3 32.6 reduce-scatter.3
  223.5 49.1 reduce-scatter.5
  275.1 49.0 reduce-scatter.7
Sparse Core Ops, SparseCore 1:
  289.6 81.6 all-gather.10

commit v2 on v1

v2 whole, which is shorter than its diff:
```python
import math

import jax
import jax.numpy as jnp
from jax import lax
from jax.experimental import pallas as pl
from jax.experimental.pallas import tpu as pltpu
from jax.sharding import PartitionSpec as P

CHUNKS = (3, 2)
VMEM = 58 * 2**20


def shift(x, by):
    size = lax.axis_size("dp")
    return lax.ppermute(x, "dp", [(i, (i + by) % size) for i in range(size)])


def pick_ranks(ids):
    rows = ids.shape[0]
    earlier = jnp.arange(rows)[None, :] < jnp.arange(rows)[:, None]
    same = ids[:, :, None, None] == ids[None, None, :, :]
    return jnp.sum((same & earlier[:, None, :, None]).astype(jnp.int32), axis=(2, 3))


def gather_neighbours(own):
    top, end = own
    left_top, right_end = shift(top, 1), shift(end, -1)
    left_end, right_top = shift(end, 1), shift(top, -1)
    return left_top, left_end, right_top, right_end


def hidden_kernel(steps, place_ref, *refs):
    rows, (gate_ref, up_ref, out_ref, gate_sum, up_sum) = refs[:8], refs[8:]
    size = 2 * rows[0].shape[0]
    step = pl.program_id(0)

    @pl.when(step == 0)
    def _():
        gate_sum[...] = jnp.zeros_like(gate_sum)
        up_sum[...] = jnp.zeros_like(up_sum)

    x = jnp.concatenate([r[...] for r in rows], axis=0)
    gate_sum[...] += jnp.dot(x, gate_ref[0], preferred_element_type=jnp.float32)
    up_sum[...] += jnp.dot(x, up_ref[0], preferred_element_type=jnp.float32)

    @pl.when(step == steps - 1)
    def _():
        for i, by in enumerate((0, 3, 1, 2)):
            part = pl.ds(i * size, size)
            gate = gate_sum[part, :]
            act = gate / (1.0 + jnp.exp(-gate)) * up_sum[part, :]
            start = pl.multiple_of(lax.rem(place_ref[0] + by, 4) * size, size)
            out_ref[pl.ds(start, size), :] = act.astype(out_ref.dtype)


def hidden_units(rows, w_gate, w_up):
    half, width = rows[0].shape
    hidden = w_gate.shape[2]
    block = 1024
    steps = width // block
    total = 8 * half
    place = lax.axis_index("dp").astype(jnp.int32).reshape(1)
    return pl.pallas_call(
        lambda *refs: hidden_kernel(steps, *refs),
        grid_spec=pltpu.PrefetchScalarGridSpec(
            num_scalar_prefetch=1,
            grid=(steps,),
            in_specs=[pl.BlockSpec((half, block), lambda i, p: (0, i))] * 8
            + [pl.BlockSpec((1, block, hidden), lambda i, p: (0, i, 0))] * 2,
            out_specs=pl.BlockSpec((total, hidden), lambda i, p: (0, 0)),
            scratch_shapes=[pltpu.VMEM((total, hidden), jnp.float32)] * 2,
        ),
        out_shape=jax.ShapeDtypeStruct((total, hidden), jnp.bfloat16),
        compiler_params=pltpu.CompilerParams(vmem_limit_bytes=VMEM),
        cost_estimate=pl.CostEstimate(
            flops=4 * total * width * hidden,
            bytes_accessed=2 * (2 * width * hidden + total * width),
            transcendentals=total * hidden,
        ),
    )(place, *rows, w_gate, w_up)


def down_kernel(*refs):
    acts, downs, out_ref = refs[:4], refs[4:8], refs[8]
    out = jnp.dot(acts[0][...], downs[0][...], preferred_element_type=jnp.float32)
    for act, down in zip(acts[1:], downs[1:]):
        out += jnp.dot(act[...], down[...], preferred_element_type=jnp.float32)
    out_ref[...] = out.astype(out_ref.dtype)


def down_product(acts, downs):
    rows, hidden = acts[0].shape
    width = downs[0].shape[1]
    block = 256
    return pl.pallas_call(
        down_kernel,
        grid=(width // block,),
        in_specs=[pl.BlockSpec((rows, hidden), lambda i: (0, 0))] * 4
        + [pl.BlockSpec((hidden, block), lambda i: (0, i))] * 4,
        out_specs=pl.BlockSpec((rows, block), lambda i: (0, i)),
        out_shape=jax.ShapeDtypeStruct((rows, width), jnp.bfloat16),
        compiler_params=pltpu.CompilerParams(vmem_limit_bytes=VMEM),
        cost_estimate=pl.CostEstimate(
            flops=8 * rows * hidden * width,
            bytes_accessed=2 * (4 * hidden * width + rows * width + 4 * rows * hidden),
            transcendentals=0,
        ),
    )(*acts, *downs)


def shards(tokens, expert_ids, gate_values, pair_order, w_gate, w_up, w_down, sketch):
    rows_dev, width = tokens.shape
    experts = lax.axis_size("expert")
    groups = lax.axis_size("dp")
    lanes = 128
    tall = width // lanes
    ranks = pick_ranks(expert_ids)

    def place_of(first, count):
        inside = (ranks >= first) & (ranks < first + count)
        return jnp.where(inside, expert_ids * count + ranks - first, -1)

    places, first = [], 0
    for count in CHUNKS:
        places.append(place_of(first, count))
        first += count

    place = lax.axis_index("dp")
    columns = width // groups

    def down_columns(by):
        start = lax.rem(place + by, groups) * columns
        return lax.dynamic_slice_in_dim(w_down[0], start, columns, axis=1)

    down_parts = tuple(down_columns(by) for by in (0, 1, groups - 1, 2))
    full_sketch = lax.all_gather(sketch, "expert", axis=0, tiled=True)

    arrived = []
    for i, (count, place) in enumerate(zip(CHUNKS, places)):
        spots = jnp.arange(experts * count, dtype=jnp.int32)
        select = jnp.any(place[None, :, :] == spots[:, None, None], axis=2)
        placed = jnp.dot(select.astype(jnp.bfloat16), tokens, preferred_element_type=jnp.float32)
        outgoing = placed.astype(jnp.bfloat16).reshape(experts, count * tall, lanes)
        if i == 0:
            outgoing, down_parts = lax.optimization_barrier((outgoing, down_parts))
            downs = tuple(shift(part, by) if by else part for part, by in zip(down_parts, (0, 1, -1, 2)))
        elif i == 1:
            outgoing, downs = lax.optimization_barrier((outgoing, downs))
        incoming = lax.all_to_all(outgoing, "expert", split_axis=0, concat_axis=0, tiled=True)
        arrived.append(incoming)

    middle = experts // 2
    last = len(CHUNKS) - 1
    owns, firsts, seconds = [], [], []
    for i, count in enumerate(CHUNKS):
        parts = (arrived[i][:middle], arrived[i][middle:])
        own = tuple(part.reshape(middle * count, width) for part in parts)
        first = gather_neighbours(own)
        if i < last:
            first, arrived[i + 1] = lax.optimization_barrier((first, arrived[i + 1]))
        owns.append(own)
        firsts.append(first)
        seconds.append((shift(first[0], 1), shift(first[3], -1)))

    acts, outs = [], []

    done = full_sketch
    for i in range(len(CHUNKS)):
        second = seconds[i]
        if i < last:
            second, firsts[i + 1], done = lax.optimization_barrier((second, firsts[i + 1], done))
            seconds[i + 1] = (shift(firsts[i + 1][0], 1), shift(firsts[i + 1][3], -1))
        else:
            second, done = lax.optimization_barrier((second, done))
        if i == 0:
            full_sketch = done
        elif i > 1:
            outs[i - 2] = done
        act = hidden_units((*owns[i], *firsts[i], *second), w_gate, w_up)
        sent = (act, shift(act, 1), shift(act, -1), shift(act, 2))
        acts.append(sent)
        if i:
            acts[i - 1], act = lax.optimization_barrier((acts[i - 1], act))
            acts[i] = (act, *acts[i][1:])
            outs.append(down_product(acts[i - 1], downs))
            done = outs[i - 1]
        else:
            done = ()
    acts[last], outs[last - 1] = lax.optimization_barrier((acts[last], outs[last - 1]))
    outs.append(down_product(acts[last], downs))

    mixed_sum = jnp.zeros((groups, rows_dev, columns), jnp.float32)
    back = ()
    for count, place, out in zip(CHUNKS, places, outs):
        out = out.reshape(groups * experts, count * (columns // lanes), lanes)
        out, back = lax.optimization_barrier((out, back))
        back = lax.all_to_all(out, ("dp", "expert"), split_axis=0, concat_axis=0, tiled=True)
        back = back.reshape(groups, experts * count, columns)
        spots = jnp.arange(experts * count, dtype=jnp.int32)
        matches = place[:, :, None] == spots[None, None, :]
        weights = jnp.sum(
            jnp.where(matches, gate_values[:, :, None], jnp.zeros((), jnp.bfloat16)), axis=1
        )
        mixed_sum = mixed_sum + jnp.einsum(
            "ts,gsc->gtc", weights, back, preferred_element_type=jnp.float32
        )
    mixed_parts = mixed_sum.astype(jnp.bfloat16)
    mixed = jnp.transpose(mixed_parts, (1, 0, 2)).reshape(rows_dev, width)

    pairs = rows_dev // 2
    order = pair_order[0].reshape(pairs, 2)
    row_ids = jnp.arange(rows_dev, dtype=jnp.int32)
    signs = (order[:, 0:1] == row_ids[None, :]).astype(jnp.bfloat16) - (
        order[:, 1:2] == row_ids[None, :]
    ).astype(jnp.bfloat16)
    contrast = jnp.einsum("pt,gtc->gpc", signs, mixed_parts, preferred_element_type=jnp.float32)
    contrast = contrast.astype(jnp.bfloat16)
    sent = lax.all_to_all(contrast, "dp", split_axis=0, concat_axis=0, tiled=True)
    projected = jnp.einsum(
        "gpc,gck->pk",
        contrast,
        full_sketch.reshape(groups, columns, -1),
        preferred_element_type=jnp.float32,
    ).astype(jnp.bfloat16)
    nearby = (projected, shift(projected, -1), shift(projected, 2), shift(projected, 1))
    here = lax.axis_index("dp")
    projected = jnp.concatenate(
        [
            lax.select_n(lax.rem(g - here + groups, groups), *nearby)
            for g in range(groups)
        ],
        axis=0,
    )
    covariance = lax.dot_general(
        sent.reshape(groups * pairs, columns),
        projected,
        (((0,), (0,)), ((), ())),
        preferred_element_type=jnp.float32,
    )
    parts = covariance.astype(jnp.bfloat16).reshape(experts, -1, covariance.shape[1])
    parts = lax.all_to_all(parts, "expert", split_axis=0, concat_axis=0, tiled=True)
    reading = jnp.sum(parts.astype(jnp.float32), axis=0)
    reading = reading * (1.0 / math.sqrt(pairs * groups * experts))
    return (mixed, reading)


def solution(mesh):
    return jax.shard_map(
        shards,
        mesh=mesh,
        in_specs=(
            P(("dp", "expert"), None),
            P(("dp", "expert"), None),
            P(("dp", "expert"), None),
            P(("dp", "expert"), None),
            P("expert", None, "dp"),
            P("expert", None, "dp"),
            P("expert", "dp", None),
            P("expert", None),
        ),
        out_specs=(P(("dp", "expert"), None), P(("dp", "expert"), None)),
        check_vma=False,
    )
```

time: 433 us -> 371 us (0.86)
  blocking collectives: 138 us -> 0 us
  matrix products: 60.3 us -> 10.8 us
  starting transfers between devices: 37.4 us -> 86.5 us
  waiting for transfers between devices: 153 us -> 197 us
  Pallas kernels: 0 us -> 32.4 us
    all_to_all x4 -> x0, blocking collectives: 127 us -> none  [the longest x3 100 us: shards(): lax.all_to_all(outgoing, 'expert', split_axis=0, concat_axis=0, tiled=True)]
    reduce_scatter x3 -> x0, waiting for transfers between devices: 95.5 us -> none  [shards(): lax.psum_scatter(partial.astype(jnp.bfloat16), 'dp', scatter_dimension=0,...]
    ppermute x0 -> x24, waiting for transfers between devices: none -> 90.6 us  [shift(): return lax.ppermute(x, 'dp', [(i, (i + by) % size) for i in range(size)])]
    all_to_all x4 -> x6, waiting for transfers between devices: 26.4 us -> 106 us  [the longest x2 61.9 us: shards(): lax.all_to_all(out, ('dp', 'expert'), split_axis=0, concat_axis=0, tiled=...]
    dot_general x12 -> x5, matrix products: 53.5 us -> 8.87 us  [the longest x2 4.17 us: shards(): jnp.einsum('ts,gsc->gtc', weights, back, preferred_element_type=jnp.float32)]
    pallas_call x0 -> x4, Pallas kernels: none -> 32.4 us  [the longest x2 19.3 us: hidden_units(): pl.pallas_call(lambda *refs: hidden_kernel(steps, *refs), grid_spec=pltpu...]
    all_gather x3 -> x0, waiting for transfers between devices: 30.4 us -> none  [shards(): picked = lax.all_gather(rows, 'dp', axis=0, tiled=True)]
    ppermute x0 -> x24, starting transfers between devices: none -> 30.2 us  [shift(): return lax.ppermute(x, 'dp', [(i, (i + by) % size) for i in range(size)])]
  transfers between devices with their start and end apart: 11 -> 31, of which waited for: 5 -> 16; matrix products, arithmetic and copies ran while one was open for 19% -> 5% of each run, Pallas kernels for 0% -> 9%
where the time goes in v2:
time: 371 us; the launch traced here: 370 us
  waiting for transfers between devices  197 us (53%)
  starting transfers between devices  86.5 us (23%)
  Pallas kernels  32.4 us (9%)
  local copies, waits for them, and re-layouts  26.4 us (7%)
  between operations  14.4 us (4%)
  matrix products  10.8 us (3%)
    ppermute x24, waiting for transfers between devices, shift(): return lax.ppermute(x, 'dp', [(i, (i + by) % size) for i in range(size)])  90.6 us
    all_to_all x2, waiting for transfers between devices, shards(): lax.all_to_all(out, ('dp', 'expert'), split_axis=0, concat_axis=0, tiled=...  61.9 us
    ppermute x24, starting transfers between devices, shift(): return lax.ppermute(x, 'dp', [(i, (i + by) % size) for i in range(size)])  30.2 us
    all_to_all x2, waiting for transfers between devices, shards(): lax.all_to_all(outgoing, 'expert', split_axis=0, concat_axis=0, tiled=True)  28 us
    all_to_all x2, starting transfers between devices, shards(): lax.all_to_all(out, ('dp', 'expert'), split_axis=0, concat_axis=0, tiled=...  25.6 us
    all_to_all x2, starting transfers between devices, shards(): lax.all_to_all(outgoing, 'expert', split_axis=0, concat_axis=0, tiled=True)  22.1 us
    pallas_call x2, Pallas kernels, hidden_units(): pl.pallas_call(lambda *refs: hidden_kernel(steps, *refs), grid_spec=pltpu...  19.3 us
    all_to_all x1, waiting for transfers between devices, shards(): lax.all_to_all(parts, 'expert', split_axis=0, concat_axis=0, tiled=True)  16 us
  transfers between devices with their start and end apart: 31, of which 16 were waited for; matrix products, arithmetic and copies ran while one was open for 5% of the time, Pallas kernels for 9%

profile of v2, /device:TPU:1, one launch (start us, length us, event | category | flops | bytes accessed | tf_op | source)
XLA Modules:
  0.0 370.4 jit_solution(12919009167178944003)
XLA Ops:
  9.5 2.1 reshape.74
  11.6 3.4 dynamic-slice_bitcast_fusion
  15.0 13.2 %all-to-all-start = ((bf16[64,96,128]{2,1,0:T(8,128)(2,1)}), bf16[64,96,128]{2,1,0:T(8,128)(2,1)S(1)}, u32[]{:S(2)}, u32[]{:S(2)}) async-start(bf16[64,96,128]{2,1,0:T(8,128)(2,1)} %reshape.74), calls=%async_computation | async-start | bytes 3145728 | tf_op jit(solution)/shard_map/all_to_all | solution.py:150
  29.5 1.5 collective-permute-start.5
  30.9 1.5 collective-permute-start.6
  32.5 1.4 convolution_convert_fusion.1
  33.9 2.3 reshape.77
  36.3 12.2 %collective-permute-done.4.refs_5_ = bf16[384,1024]{1,0:T(8,128)(2,1)} collective-permute-done((bf16[384,1024]{1,0:T(8,128)(2,1)}, bf16[384,1024]{1,0:T(8,128)(2,1)}, u32[]{:S(2)}, u32[]{:S(2)}) %collective-permute-start.4) | collective-permute-done | bytes 786464 | tf_op jit(solution)/shard_map/ppermute | solution.py:16
  48.4 17.8 %collective-permute-done.6.refs_7_ = bf16[384,1024]{1,0:T(8,128)(2,1)} collective-permute-done((bf16[384,1024]{1,0:T(8,128)(2,1)S(1)}, bf16[384,1024]{1,0:T(8,128)(2,1)}, u32[]{:S(2)}, u32[]{:S(2)}) %collective-permute-start.6) | collective-permute-done | bytes 786464 | tf_op jit(solution)/shard_map/ppermute | solution.py:16
  66.3 2.5 all-to-all-done
  68.8 8.9 %all-to-all-start.1 = ((bf16[64,64,128]{2,1,0:T(8,128)(2,1)}), bf16[64,64,128]{2,1,0:T(8,128)(2,1)}, u32[]{:S(2)}, u32[]{:S(2)}) async-start(bf16[64,64,128]{2,1,0:T(8,128)(2,1)} %reshape.77), calls=%async_computation.1 | async-start | bytes 2097152 | tf_op jit(solution)/shard_map/all_to_all | solution.py:150
  78.7 1.4 reshape.75.refs_1_
  81.5 2.6 collective-permute-start.2
  84.7 25.5 %all-to-all-done.1 = bf16[64,64,128]{2,1,0:T(8,128)(2,1)} async-done(((bf16[64,64,128]{2,1,0:T(8,128)(2,1)}), bf16[64,64,128]{2,1,0:T(8,128)(2,1)}, u32[]{:S(2)}, u32[]{:S(2)}) %all-to-all-start.1) | async-done | bytes 1048608 | tf_op jit(solution)/shard_map/all_to_all | solution.py:150
  110.3 7.1 %collective-permute-done.1.refs_4_ = bf16[96,4096]{1,0:T(8,128)(2,1)} collective-permute-done((bf16[96,4096]{1,0:T(8,128)(2,1)S(1)}, bf16[96,4096]{1,0:T(8,128)(2,1)}, u32[]{:S(2)}, u32[]{:S(2)}) %collective-permute-start.1) | collective-permute-done | bytes 786464 | tf_op jit(solution)/shard_map/ppermute | solution.py:16
  120.6 1.7 collective-permute-start.8
  124.1 8.1 %collective-permute-done.9.refs_3_ = bf16[64,4096]{1,0:T(8,128)(2,1)} collective-permute-done((bf16[64,4096]{1,0:T(8,128)(2,1)S(1)}, bf16[64,4096]{1,0:T(8,128)(2,1)}, u32[]{:S(2)}, u32[]{:S(2)}) %collective-permute-start.9) | collective-permute-done | bytes 524320 | tf_op jit(solution)/shard_map/ppermute | solution.py:16
  133.3 26.8 %collective-permute-done.10.refs_4_ = bf16[64,4096]{1,0:T(8,128)(2,1)S(1)} collective-permute-done((bf16[64,4096]{1,0:T(8,128)(2,1)S(1)}, bf16[64,4096]{1,0:T(8,128)(2,1)S(1)}, u32[]{:S(2)}, u32[]{:S(2)}) %collective-permute-start.10) | collective-permute-done | bytes 524320 | tf_op jit(solution)/shard_map/ppermute | solution.py:16
  162.0 1.5 collective-permute-start.17
  163.5 10.7 %shard_map.95.refs_0_ = bf16[768,384]{1,0:T(8,128)(2,1)} custom-call(s32[1]{0:T(128)} %bitcast.refs_0_, bf16[96,4096]{1,0:T(8,128)(2,1)} %copy-done.2, bf16[96,4096]{1,0:T(8,128)(2,1)} %copy-done.3, bf16[96,4096]{1,0:T(8,128)(2,1)} %copy-done.7, bf16[96,4096]{1,0:T(8,128)(2,1)} %collective-permute-done.1.refs_4_, ...), custom_call_target="tpu_custom_call" | custom-call | flops 4831838208 | bytes 12582912 | tf_op jit(solution)/shard_map/pallas_call | solution.py:64
  174.3 2.7 collective-permute-start.14
  178.5 8.6 %shard_map.96.refs_0_ = bf16[512,384]{1,0:T(8,128)(2,1)} custom-call(s32[1]{0:T(128)} %bitcast.refs_0_, bf16[64,4096]{1,0:T(8,128)(2,1)} %copy-done.4, bf16[64,4096]{1,0:T(8,128)(2,1)} %copy-done.5, bf16[64,4096]{1,0:T(8,128)(2,1)} %collective-permute-done.9.refs_3_, bf16[64,4096]{1,0:T(8,128)(2,1)} %copy-done.11, ...), custom_call_target="tpu_custom_call" | custom-call | flops 3221225472 | bytes 10485760 | tf_op jit(solution)/shard_map/pallas_call | solution.py:64
  187.7 2.1 collective-permute-start.19
  189.8 1.8 collective-permute-start.20
  191.5 6.9 %collective-permute-done.15.refs_3_ = bf16[768,384]{1,0:T(8,128)(2,1)S(1)} collective-permute-done((bf16[768,384]{1,0:T(8,128)(2,1)}, bf16[768,384]{1,0:T(8,128)(2,1)S(1)}, u32[]{:S(2)}, u32[]{:S(2)}) %collective-permute-start.15) | collective-permute-done | bytes 589856 | tf_op jit(solution)/shard_map/ppermute | solution.py:16
  199.3 7.2 %shard_map.97 = bf16[768,1024]{1,0:T(8,128)(2,1)} custom-call(bf16[768,384]{1,0:T(8,128)(2,1)} %shard_map.95.refs_0_, bf16[768,384]{1,0:T(8,128)(2,1)} %copy-done.8, bf16[768,384]{1,0:T(8,128)(2,1)} %copy-done.9, bf16[768,384]{1,0:T(8,128)(2,1)} %copy-done.10, bf16[384,1024]{1,0:T(8,128)(2,1)} %get-tuple-element.61.refs_4_, ...), custom_call_target="tpu_custom_call" | custom-call | flops 2415919104 | bytes 7077888 | tf_op jit(solution)/shard_map/pallas_call | solution.py:96
  206.4 6.1 %collective-permute-done.18.refs_1_ = bf16[512,384]{1,0:T(8,128)(2,1)} collective-permute-done((bf16[512,384]{1,0:T(8,128)(2,1)}, bf16[512,384]{1,0:T(8,128)(2,1)}, u32[]{:S(2)}, u32[]{:S(2)}) %collective-permute-start.18) | collective-permute-done | bytes 393248 | tf_op jit(solution)/shard_map/ppermute | solution.py:16
  212.5 2.6 collective-permute-done.20.refs_3_
  215.1 3.7 reshape.80
  218.8 18.7 %all-to-all-start.2 = ((bf16[256,24,128]{2,1,0:T(8,128)(2,1)}), bf16[256,24,128]{2,1,0:T(8,128)(2,1)S(1)}, u32[]{:S(2)}, u32[]{:S(2)}) async-start(bf16[256,24,128]{2,1,0:T(8,128)(2,1)} %reshape.80), calls=%async_computation.2 | async-start | bytes 3145728 | tf_op jit(solution)/shard_map/all_to_all | solution.py:198
  237.5 6.0 %shard_map.98 = bf16[512,1024]{1,0:T(8,128)(2,1)} custom-call(bf16[512,384]{1,0:T(8,128)(2,1)} %shard_map.96.refs_0_, bf16[512,384]{1,0:T(8,128)(2,1)} %collective-permute-done.18.refs_1_, bf16[512,384]{1,0:T(8,128)(2,1)} %collective-permute-done.19.refs_2_, bf16[512,384]{1,0:T(8,128)(2,1)} %collective-permute-done.20.refs_3_, ...), custom_call_target="tpu_custom_call" | custom-call | flops 1610612736 | bytes 5767168 | tf_op jit(solution)/shard_map/pallas_call | solution.py:96
  243.5 2.3 reshape.82
  245.8 35.5 %all-to-all-done.2 = bf16[256,24,128]{2,1,0:T(8,128)(2,1)S(1)} async-done(((bf16[256,24,128]{2,1,0:T(8,128)(2,1)}), bf16[256,24,128]{2,1,0:T(8,128)(2,1)S(1)}, u32[]{:S(2)}, u32[]{:S(2)}) %all-to-all-start.2) | async-done | bytes 1572896 | tf_op jit(solution)/shard_map/all_to_all | solution.py:198
  281.3 2.1 reshape.81
  283.4 7.0 %all-to-all-start.3 = ((bf16[256,16,128]{2,1,0:T(8,128)(2,1)}), bf16[256,16,128]{2,1,0:T(8,128)(2,1)}, u32[]{:S(2)}, u32[]{:S(2)}) async-start(bf16[256,16,128]{2,1,0:T(8,128)(2,1)} %reshape.82), calls=%async_computation.3 | async-start | bytes 2097152 | tf_op jit(solution)/shard_map/all_to_all | solution.py:198
  292.0 2.1 fusion.16
  294.1 26.4 %all-to-all-done.3 = bf16[256,16,128]{2,1,0:T(8,128)(2,1)} async-done(((bf16[256,16,128]{2,1,0:T(8,128)(2,1)}), bf16[256,16,128]{2,1,0:T(8,128)(2,1)}, u32[]{:S(2)}, u32[]{:S(2)}) %all-to-all-start.3) | async-done | bytes 1048608 | tf_op jit(solution)/shard_map/all_to_all | solution.py:198
  320.5 1.5 reshape.83
  322.1 2.1 add_convert_fusion
  324.1 1.3 fusion
  325.5 3.5 all-to-all-start.4
  328.9 2.2 fusion.1
  331.2 3.0 collective-permute-start.22
  334.5 2.4 collective-permute-start.21
  336.9 2.0 collective-permute-done.22
  340.5 5.0 %all-to-all-start.5 = ((bf16[64,16,256]{2,1,0:T(8,128)(2,1)}), bf16[64,16,256]{2,1,0:T(8,128)(2,1)S(1)}, u32[]{:S(2)}, u32[]{:S(2)}) async-start(bf16[64,16,256]{2,1,0:T(8,128)(2,1)} %bitcast.15), calls=%async_computation.5 | async-start | bytes 1048576 | tf_op jit(solution)/shard_map/all_to_all | solution.py:242
  345.5 1.3 copy.33
  346.8 16.0 %all-to-all-done.5 = bf16[64,16,256]{2,1,0:T(8,128)(2,1)S(1)} async-done(((bf16[64,16,256]{2,1,0:T(8,128)(2,1)}), bf16[64,16,256]{2,1,0:T(8,128)(2,1)S(1)}, u32[]{:S(2)}, u32[]{:S(2)}) %all-to-all-start.5) | async-done | bytes 524320 | tf_op jit(solution)/shard_map/all_to_all | solution.py:242
  (84 shorter events, 21.9 us)
Async XLA Ops:
  7.2 1.7 copy-start
  15.0 53.9 %all-to-all-start = ((bf16[64,96,128]{2,1,0:T(8,128)(2,1)}), bf16[64,96,128]{2,1,0:T(8,128)(2,1)S(1)}, u32[]{:S(2)}, u32[]{:S(2)}) async-start(bf16[64,96,128]{2,1,0:T(8,128)(2,1)} %reshape.74), calls=%async_computation | async-start | bytes 3145728 | tf_op jit(solution)/shard_map/all_to_all | solution.py:150
  28.1 105.2 %all-gather.2.cloned.1.call-start = ((), (), s32[]{:S(2)}) async-start(), calls=%async_computation.6 | async-start | bytes 2129920 | tf_op jit(solution)/shard_map/all_gather | solution.py:137
  28.2 20.3 %collective-permute-start.4 = (bf16[384,1024]{1,0:T(8,128)(2,1)}, bf16[384,1024]{1,0:T(8,128)(2,1)}, u32[]{:S(2)}, u32[]{:S(2)}) collective-permute-start(bf16[384,1024]{1,0:T(8,128)(2,1)} %get-tuple-element.39), channel_id=1, source_target_pairs={{0,64},{64,128},{128,192},{192,0},{1,65},{65,129},{129,193},{193,1... | collective-permute-start | bytes 2359304 | tf_op jit(solution)/shard_map/ppermute | solution.py:16
  29.5 19.0 %collective-permute-start.5 = (bf16[384,1024]{1,0:T(8,128)(2,1)}, bf16[384,1024]{1,0:T(8,128)(2,1)}, u32[]{:S(2)}, u32[]{:S(2)}) collective-permute-start(bf16[384,1024]{1,0:T(8,128)(2,1)} %get-tuple-element.40), channel_id=1, source_target_pairs={{0,192},{64,0},{128,64},{192,128},{1,193},{65,1},{129,65},{193,129... | collective-permute-start | bytes 2359304 | tf_op jit(solution)/shard_map/ppermute | solution.py:16
  30.9 35.3 %collective-permute-start.6 = (bf16[384,1024]{1,0:T(8,128)(2,1)S(1)}, bf16[384,1024]{1,0:T(8,128)(2,1)}, u32[]{:S(2)}, u32[]{:S(2)}) collective-permute-start(bf16[384,1024]{1,0:T(8,128)(2,1)S(1)} %get-tuple-element.41), channel_id=1, source_target_pairs={{0,128},{64,192},{128,0},{192,64},{1,129},{65,193},{129,1},{193,65... | collective-permute-start | bytes 2359304 | tf_op jit(solution)/shard_map/ppermute | solution.py:16
  68.8 41.4 %all-to-all-start.1 = ((bf16[64,64,128]{2,1,0:T(8,128)(2,1)}), bf16[64,64,128]{2,1,0:T(8,128)(2,1)}, u32[]{:S(2)}, u32[]{:S(2)}) async-start(bf16[64,64,128]{2,1,0:T(8,128)(2,1)} %reshape.77), calls=%async_computation.1 | async-start | bytes 2097152 | tf_op jit(solution)/shard_map/all_to_all | solution.py:150
  80.2 37.2 %copy-start.2 = (bf16[96,4096]{1,0:T(8,128)(2,1)}, bf16[96,4096]{1,0:T(8,128)(2,1)S(1)}, u32[]{:S(2)}) copy-start(bf16[96,4096]{1,0:T(8,128)(2,1)S(1)} %reshape.75.refs_1_) | copy-start | bytes 2359300
  80.5 36.8 %copy-start.3 = (bf16[96,4096]{1,0:T(8,128)(2,1)}, bf16[96,4096]{1,0:T(8,128)(2,1)S(1)}, u32[]{:S(2)}) copy-start(bf16[96,4096]{1,0:T(8,128)(2,1)S(1)} %reshape.76.refs_2_) | copy-start | bytes 2359300
  80.5 29.7 %collective-permute-start = (bf16[96,4096]{1,0:T(8,128)(2,1)S(1)}, bf16[96,4096]{1,0:T(8,128)(2,1)S(1)}, u32[]{:S(2)}, u32[]{:S(2)}) collective-permute-start(bf16[96,4096]{1,0:T(8,128)(2,1)S(1)} %reshape.75.refs_1_), channel_id=1, source_target_pairs={{0,64},{64,128},{128,192},{192,0},{1,65},{65,129},{129,193},{193,1... | collective-permute-start | bytes 2359304 | tf_op jit(solution)/shard_map/ppermute | solution.py:16
  81.5 35.9 %collective-permute-start.1 = (bf16[96,4096]{1,0:T(8,128)(2,1)S(1)}, bf16[96,4096]{1,0:T(8,128)(2,1)}, u32[]{:S(2)}, u32[]{:S(2)}) collective-permute-start(bf16[96,4096]{1,0:T(8,128)(2,1)S(1)} %reshape.76.refs_2_), channel_id=1, source_target_pairs={{0,64},{64,128},{128,192},{192,0},{1,65},{65,129},{129,193},{193,1... | collective-permute-start | bytes 2359304 | tf_op jit(solution)/shard_map/ppermute | solution.py:16
  81.5 35.8 %collective-permute-start.2 = (bf16[96,4096]{1,0:T(8,128)(2,1)S(1)}, bf16[96,4096]{1,0:T(8,128)(2,1)}, u32[]{:S(2)}, u32[]{:S(2)}) collective-permute-start(bf16[96,4096]{1,0:T(8,128)(2,1)S(1)} %reshape.75.refs_1_), channel_id=1, source_target_pairs={{0,192},{64,0},{128,64},{192,128},{1,193},{65,1},{129,65},{193,129... | collective-permute-start | bytes 2359304 | tf_op jit(solution)/shard_map/ppermute | solution.py:16
  84.1 33.2 %collective-permute-start.3 = (bf16[96,4096]{1,0:T(8,128)(2,1)S(1)}, bf16[96,4096]{1,0:T(8,128)(2,1)}, u32[]{:S(2)}, u32[]{:S(2)}) collective-permute-start(bf16[96,4096]{1,0:T(8,128)(2,1)S(1)} %reshape.76.refs_2_), channel_id=1, source_target_pairs={{0,192},{64,0},{128,64},{192,128},{1,193},{65,1},{129,65},{193,129... | collective-permute-start | bytes 2359304 | tf_op jit(solution)/shard_map/ppermute | solution.py:16
  110.3 13.4 %copy-start.7 = (bf16[96,4096]{1,0:T(8,128)(2,1)}, bf16[96,4096]{1,0:T(8,128)(2,1)S(1)}, u32[]{:S(2)}) copy-start(bf16[96,4096]{1,0:T(8,128)(2,1)S(1)} %collective-permute-done.refs_3_) | copy-start | bytes 2359300
  118.9 55.3 %copy-start.4 = (bf16[64,4096]{1,0:T(8,128)(2,1)}, bf16[64,4096]{1,0:T(8,128)(2,1)S(1)}, u32[]{:S(2)}) copy-start(bf16[64,4096]{1,0:T(8,128)(2,1)S(1)} %reshape.78.refs_1_) | copy-start | bytes 1572868
  118.9 13.3 %collective-permute-start.9 = (bf16[64,4096]{1,0:T(8,128)(2,1)S(1)}, bf16[64,4096]{1,0:T(8,128)(2,1)}, u32[]{:S(2)}, u32[]{:S(2)}) collective-permute-start(bf16[64,4096]{1,0:T(8,128)(2,1)S(1)} %reshape.78.refs_1_), channel_id=1, source_target_pairs={{0,64},{64,128},{128,192},{192,0},{1,65},{65,129},{129,193},{193,1... | collective-permute-start | bytes 1572872 | tf_op jit(solution)/shard_map/ppermute | solution.py:16
  119.6 41.1 %collective-permute-start.7 = (bf16[96,4096]{1,0:T(8,128)(2,1)S(1)}, bf16[96,4096]{1,0:T(8,128)(2,1)}, u32[]{:S(2)}, u32[]{:S(2)}) collective-permute-start(bf16[96,4096]{1,0:T(8,128)(2,1)S(1)} %collective-permute-done.refs_3_), channel_id=1, source_target_pairs={{0,64},{64,128},{128,192},{192,0},{1,65},{65,129},{129,193},{193,1... | collective-permute-start | bytes 2359304 | tf_op jit(solution)/shard_map/ppermute | solution.py:16
  120.6 40.1 %collective-permute-start.8 = (bf16[96,4096]{1,0:T(8,128)(2,1)}, bf16[96,4096]{1,0:T(8,128)(2,1)}, u32[]{:S(2)}, u32[]{:S(2)}) collective-permute-start(bf16[96,4096]{1,0:T(8,128)(2,1)} %collective-permute-done.3.refs_6_), channel_id=1, source_target_pairs={{0,192},{64,0},{128,64},{192,128},{1,193},{65,1},{129,65},{193,129... | collective-permute-start | bytes 2359304 | tf_op jit(solution)/shard_map/ppermute | solution.py:16
  122.3 37.8 %collective-permute-start.11 = (bf16[64,4096]{1,0:T(8,128)(2,1)S(1)}, bf16[64,4096]{1,0:T(8,128)(2,1)}, u32[]{:S(2)}, u32[]{:S(2)}) collective-permute-start(bf16[64,4096]{1,0:T(8,128)(2,1)S(1)} %reshape.78.refs_1_), channel_id=1, source_target_pairs={{0,192},{64,0},{128,64},{192,128},{1,193},{65,1},{129,65},{193,129... | collective-permute-start | bytes 1572872 | tf_op jit(solution)/shard_map/ppermute | solution.py:16
  123.6 50.5 %copy-start.5 = (bf16[64,4096]{1,0:T(8,128)(2,1)}, bf16[64,4096]{1,0:T(8,128)(2,1)S(1)}, u32[]{:S(2)}) copy-start(bf16[64,4096]{1,0:T(8,128)(2,1)S(1)} %reshape.79.refs_2_) | copy-start | bytes 1572868
  123.6 36.5 %collective-permute-start.10 = (bf16[64,4096]{1,0:T(8,128)(2,1)S(1)}, bf16[64,4096]{1,0:T(8,128)(2,1)S(1)}, u32[]{:S(2)}, u32[]{:S(2)}) collective-permute-start(bf16[64,4096]{1,0:T(8,128)(2,1)S(1)} %reshape.79.refs_2_), channel_id=1, source_target_pairs={{0,64},{64,128},{128,192},{192,0},{1,65},{65,129},{129,193},{193,1... | collective-permute-start | bytes 1572872 | tf_op jit(solution)/shard_map/ppermute | solution.py:16
  132.2 28.6 %collective-permute-start.12 = (bf16[64,4096]{1,0:T(8,128)(2,1)S(1)}, bf16[64,4096]{1,0:T(8,128)(2,1)}, u32[]{:S(2)}, u32[]{:S(2)}) collective-permute-start(bf16[64,4096]{1,0:T(8,128)(2,1)S(1)} %reshape.79.refs_2_), channel_id=1, source_target_pairs={{0,192},{64,0},{128,64},{192,128},{1,193},{65,1},{129,65},{193,129... | collective-permute-start | bytes 1572872 | tf_op jit(solution)/shard_map/ppermute | solution.py:16
  160.2 14.0 %copy-start.11 = (bf16[64,4096]{1,0:T(8,128)(2,1)}, bf16[64,4096]{1,0:T(8,128)(2,1)S(1)}, u32[]{:S(2)}) copy-start(bf16[64,4096]{1,0:T(8,128)(2,1)S(1)} %collective-permute-done.10.refs_4_) | copy-start | bytes 1572868
  160.8 16.2 %collective-permute-start.16 = (bf16[64,4096]{1,0:T(8,128)(2,1)}, bf16[64,4096]{1,0:T(8,128)(2,1)S(1)}, u32[]{:S(2)}, u32[]{:S(2)}) collective-permute-start(bf16[64,4096]{1,0:T(8,128)(2,1)} %collective-permute-done.9.refs_3_), channel_id=1, source_target_pairs={{0,64},{64,128},{128,192},{192,0},{1,65},{65,129},{129,193},{193,1... | collective-permute-start | bytes 1572872 | tf_op jit(solution)/shard_map/ppermute | solution.py:16
  162.0 15.0 %collective-permute-start.17 = (bf16[64,4096]{1,0:T(8,128)(2,1)}, bf16[64,4096]{1,0:T(8,128)(2,1)S(1)}, u32[]{:S(2)}, u32[]{:S(2)}) collective-permute-start(bf16[64,4096]{1,0:T(8,128)(2,1)} %collective-permute-done.12.refs_6_), channel_id=1, source_target_pairs={{0,192},{64,0},{128,64},{192,128},{1,193},{65,1},{129,65},{193,129... | collective-permute-start | bytes 1572872 | tf_op jit(solution)/shard_map/ppermute | solution.py:16
  174.2 15.6 %collective-permute-start.13 = (bf16[768,384]{1,0:T(8,128)(2,1)}, bf16[768,384]{1,0:T(8,128)(2,1)S(1)}, u32[]{:S(2)}, u32[]{:S(2)}) collective-permute-start(bf16[768,384]{1,0:T(8,128)(2,1)} %shard_map.95.refs_0_), channel_id=1, source_target_pairs={{0,64},{64,128},{128,192},{192,0},{1,65},{65,129},{129,193},{193,1... | collective-permute-start | bytes 1769480 | tf_op jit(solution)/shard_map/ppermute | solution.py:16
  174.3 17.3 %collective-permute-start.14 = (bf16[768,384]{1,0:T(8,128)(2,1)}, bf16[768,384]{1,0:T(8,128)(2,1)S(1)}, u32[]{:S(2)}, u32[]{:S(2)}) collective-permute-start(bf16[768,384]{1,0:T(8,128)(2,1)} %shard_map.95.refs_0_), channel_id=1, source_target_pairs={{0,192},{64,0},{128,64},{192,128},{1,193},{65,1},{129,65},{193,129... | collective-permute-start | bytes 1769480 | tf_op jit(solution)/shard_map/ppermute | solution.py:16
  176.9 21.5 %collective-permute-start.15 = (bf16[768,384]{1,0:T(8,128)(2,1)}, bf16[768,384]{1,0:T(8,128)(2,1)S(1)}, u32[]{:S(2)}, u32[]{:S(2)}) collective-permute-start(bf16[768,384]{1,0:T(8,128)(2,1)} %shard_map.95.refs_0_), channel_id=1, source_target_pairs={{0,128},{64,192},{128,0},{192,64},{1,129},{65,193},{129,1},{193,65... | collective-permute-start | bytes 1769480 | tf_op jit(solution)/shard_map/ppermute | solution.py:16
  176.9 0.8 copy-start.12
  177.7 0.8 copy-start.13
  187.1 25.4 %collective-permute-start.18 = (bf16[512,384]{1,0:T(8,128)(2,1)}, bf16[512,384]{1,0:T(8,128)(2,1)}, u32[]{:S(2)}, u32[]{:S(2)}) collective-permute-start(bf16[512,384]{1,0:T(8,128)(2,1)} %shard_map.96.refs_0_), channel_id=1, source_target_pairs={{0,64},{64,128},{128,192},{192,0},{1,65},{65,129},{129,193},{193,1... | collective-permute-start | bytes 1179656 | tf_op jit(solution)/shard_map/ppermute | solution.py:16
  187.7 24.8 %collective-permute-start.19 = (bf16[512,384]{1,0:T(8,128)(2,1)}, bf16[512,384]{1,0:T(8,128)(2,1)}, u32[]{:S(2)}, u32[]{:S(2)}) collective-permute-start(bf16[512,384]{1,0:T(8,128)(2,1)} %shard_map.96.refs_0_), channel_id=1, source_target_pairs={{0,192},{64,0},{128,64},{192,128},{1,193},{65,1},{129,65},{193,129... | collective-permute-start | bytes 1179656 | tf_op jit(solution)/shard_map/ppermute | solution.py:16
  189.8 8.7 %copy-start.8 = (bf16[768,384]{1,0:T(8,128)(2,1)}, bf16[768,384]{1,0:T(8,128)(2,1)S(1)}, u32[]{:S(2)}) copy-start(bf16[768,384]{1,0:T(8,128)(2,1)S(1)} %collective-permute-done.13.refs_1_) | copy-start | bytes 1769476
  189.8 25.3 %collective-permute-start.20 = (bf16[512,384]{1,0:T(8,128)(2,1)}, bf16[512,384]{1,0:T(8,128)(2,1)}, u32[]{:S(2)}, u32[]{:S(2)}) collective-permute-start(bf16[512,384]{1,0:T(8,128)(2,1)} %shard_map.96.refs_0_), channel_id=1, source_target_pairs={{0,128},{64,192},{128,0},{192,64},{1,129},{65,193},{129,1},{193,65... | collective-permute-start | bytes 1179656 | tf_op jit(solution)/shard_map/ppermute | solution.py:16
  191.5 6.9 %copy-start.9 = (bf16[768,384]{1,0:T(8,128)(2,1)}, bf16[768,384]{1,0:T(8,128)(2,1)S(1)}, u32[]{:S(2)}) copy-start(bf16[768,384]{1,0:T(8,128)(2,1)S(1)} %collective-permute-done.14.refs_2_) | copy-start | bytes 1769476
  198.5 0.8 copy-start.10
  218.8 62.5 %all-to-all-start.2 = ((bf16[256,24,128]{2,1,0:T(8,128)(2,1)}), bf16[256,24,128]{2,1,0:T(8,128)(2,1)S(1)}, u32[]{:S(2)}, u32[]{:S(2)}) async-start(bf16[256,24,128]{2,1,0:T(8,128)(2,1)} %reshape.80), calls=%async_computation.2 | async-start | bytes 3145728 | tf_op jit(solution)/shard_map/all_to_all | solution.py:198
  245.8 45.1 %copy-start.14 = (s32[1,128]{1,0:T(1,128)S(1)}, s32[1,128]{1,0:T(1,128)}, u32[]{:S(2)}) copy-start(s32[1,128]{1,0:T(1,128)} %param.11) | copy-start | bytes 1540
  245.8 46.0 %copy-start.6 = (bf16[128,2]{0,1:T(2,128)(2,1)S(1)}, bf16[128,2]{0,1:T(2,128)(2,1)}, u32[]{:S(2)}) copy-start(bf16[128,2]{0,1:T(2,128)(2,1)} %param.10) | copy-start | bytes 1540
  283.4 8.7 %copy-start.1 = (bf16[4,192,1024]{2,1,0:T(8,128)(2,1)S(1)}, bf16[4,192,1024]{2,1,0:T(8,128)(2,1)}, u32[]{:S(2)}) copy-start(bf16[4,192,1024]{2,1,0:T(8,128)(2,1)} %reshape.81) | copy-start | bytes 4718596
  283.4 37.2 %all-to-all-start.3 = ((bf16[256,16,128]{2,1,0:T(8,128)(2,1)}), bf16[256,16,128]{2,1,0:T(8,128)(2,1)}, u32[]{:S(2)}, u32[]{:S(2)}) async-start(bf16[256,16,128]{2,1,0:T(8,128)(2,1)} %reshape.82), calls=%async_computation.3 | async-start | bytes 2097152 | tf_op jit(solution)/shard_map/all_to_all | solution.py:198
  325.5 13.8 %all-to-all-start.4 = ((bf16[4,64,1024]{2,1,0:T(8,128)(2,1)}), bf16[4,64,1024]{2,1,0:T(8,128)(2,1)S(1)}, u32[]{:S(2)}, u32[]{:S(2)}) async-start(bf16[4,64,1024]{2,1,0:T(8,128)(2,1)} %fusion), calls=%async_computation.4 | async-start | bytes 1048576 | tf_op jit(solution)/shard_map/all_to_all | solution.py:219
  331.2 7.7 %collective-permute-start.22 = (bf16[64,256]{1,0:T(8,128)(2,1)S(1)}, bf16[64,256]{1,0:T(8,128)(2,1)S(1)}, u32[]{:S(2)}, u32[]{:S(2)}) collective-permute-start(bf16[64,256]{1,0:T(8,128)(2,1)S(1)} %fusion.1), channel_id=1, source_target_pairs={{0,128},{64,192},{128,0},{192,64},{1,129},{65,193},{129,1},{193,65... | collective-permute-start | bytes 98312 | tf_op jit(solution)/shard_map/ppermute | solution.py:16
  334.2 5.1 %collective-permute-start.23 = (bf16[64,256]{1,0:T(8,128)(2,1)S(1)}, bf16[64,256]{1,0:T(8,128)(2,1)S(1)}, u32[]{:S(2)}, u32[]{:S(2)}) collective-permute-start(bf16[64,256]{1,0:T(8,128)(2,1)S(1)} %fusion.1), channel_id=1, source_target_pairs={{0,64},{64,128},{128,192},{192,0},{1,65},{65,129},{129,193},{193,1... | collective-permute-start | bytes 98312 | tf_op jit(solution)/shard_map/ppermute | solution.py:16
  334.5 4.8 %collective-permute-start.21 = (bf16[64,256]{1,0:T(8,128)(2,1)S(1)}, bf16[64,256]{1,0:T(8,128)(2,1)S(1)}, u32[]{:S(2)}, u32[]{:S(2)}) collective-permute-start(bf16[64,256]{1,0:T(8,128)(2,1)S(1)} %fusion.1), channel_id=1, source_target_pairs={{0,192},{64,0},{128,64},{192,128},{1,193},{65,1},{129,65},{193,129... | collective-permute-start | bytes 98312 | tf_op jit(solution)/shard_map/ppermute | solution.py:16
  340.5 22.3 %all-to-all-start.5 = ((bf16[64,16,256]{2,1,0:T(8,128)(2,1)}), bf16[64,16,256]{2,1,0:T(8,128)(2,1)S(1)}, u32[]{:S(2)}, u32[]{:S(2)}) async-start(bf16[64,16,256]{2,1,0:T(8,128)(2,1)} %bitcast.15), calls=%async_computation.5 | async-start | bytes 1048576 | tf_op jit(solution)/shard_map/all_to_all | solution.py:242
Sparse Core Ops, SparseCore 0:
  32.6 81.5 all-gather.1

commit v3 on v2

--- a/solution.py
+++ b/solution.py
@@ -86,20 +86,21 @@
     out = jnp.dot(acts[0][...], downs[0][...], preferred_element_type=jnp.float32)
     for act, down in zip(acts[1:], downs[1:]):
         out += jnp.dot(act[...], down[...], preferred_element_type=jnp.float32)
-    out_ref[...] = out.astype(out_ref.dtype)
+    out_ref[...] = out.reshape(out_ref.shape).astype(out_ref.dtype)
 
 
 def down_product(acts, downs):
     rows, hidden = acts[0].shape
     width = downs[0].shape[1]
     block = 256
+    tall = width // 128
     return pl.pallas_call(
         down_kernel,
-        grid=(width // block,),
-        in_specs=[pl.BlockSpec((rows, hidden), lambda i: (0, 0))] * 4
-        + [pl.BlockSpec((hidden, block), lambda i: (0, i))] * 4,
-        out_specs=pl.BlockSpec((rows, block), lambda i: (0, i)),
-        out_shape=jax.ShapeDtypeStruct((rows, width), jnp.bfloat16),
+        grid=(rows // block,),
+        in_specs=[pl.BlockSpec((block, hidden), lambda i: (i, 0))] * 4
+        + [pl.BlockSpec((hidden, width), lambda i: (0, 0))] * 4,
+        out_specs=pl.BlockSpec((block, tall, 128), lambda i: (i, 0, 0)),
+        out_shape=jax.ShapeDtypeStruct((rows, tall, 128), jnp.bfloat16),
         compiler_params=pltpu.CompilerParams(vmem_limit_bytes=VMEM),
         cost_estimate=pl.CostEstimate(
             flops=8 * rows * hidden * width,
@@ -134,61 +135,51 @@
         return lax.dynamic_slice_in_dim(w_down[0], start, columns, axis=1)
 
     down_parts = tuple(down_columns(by) for by in (0, 1, groups - 1, 2))
-    full_sketch = lax.all_gather(sketch, "expert", axis=0, tiled=True)
-
-    arrived = []
-    for i, (count, place) in enumerate(zip(CHUNKS, places)):
+    def outgoing_rows(count, place):
         spots = jnp.arange(experts * count, dtype=jnp.int32)
         select = jnp.any(place[None, :, :] == spots[:, None, None], axis=2)
         placed = jnp.dot(select.astype(jnp.bfloat16), tokens, preferred_element_type=jnp.float32)
-        outgoing = placed.astype(jnp.bfloat16).reshape(experts, count * tall, lanes)
-        if i == 0:
-            outgoing, down_parts = lax.optimization_barrier((outgoing, down_parts))
-            downs = tuple(shift(part, by) if by else part for part, by in zip(down_parts, (0, 1, -1, 2)))
-        elif i == 1:
-            outgoing, downs = lax.optimization_barrier((outgoing, downs))
-        incoming = lax.all_to_all(outgoing, "expert", split_axis=0, concat_axis=0, tiled=True)
-        arrived.append(incoming)
-
-    middle = experts // 2
-    last = len(CHUNKS) - 1
-    owns, firsts, seconds = [], [], []
-    for i, count in enumerate(CHUNKS):
-        parts = (arrived[i][:middle], arrived[i][middle:])
-        own = tuple(part.reshape(middle * count, width) for part in parts)
-        first = gather_neighbours(own)
-        if i < last:
-            first, arrived[i + 1] = lax.optimization_barrier((first, arrived[i + 1]))
-        owns.append(own)
-        firsts.append(first)
-        seconds.append((shift(first[0], 1), shift(first[3], -1)))
-
-    acts, outs = [], []
-
-    done = full_sketch
-    for i in range(len(CHUNKS)):
-        second = seconds[i]
-        if i < last:
-            second, firsts[i + 1], done = lax.optimization_barrier((second, firsts[i + 1], done))
-            seconds[i + 1] = (shift(firsts[i + 1][0], 1), shift(firsts[i + 1][3], -1))
-        else:
-            second, done = lax.optimization_barrier((second, done))
-        if i == 0:
-            full_sketch = done
-        elif i > 1:
-            outs[i - 2] = done
-        act = hidden_units((*owns[i], *firsts[i], *second), w_gate, w_up)
-        sent = (act, shift(act, 1), shift(act, -1), shift(act, 2))
-        acts.append(sent)
-        if i:
-            acts[i - 1], act = lax.optimization_barrier((acts[i - 1], act))
-            acts[i] = (act, *acts[i][1:])
-            outs.append(down_product(acts[i - 1], downs))
-            done = outs[i - 1]
-        else:
-            done = ()
-    acts[last], outs[last - 1] = lax.optimization_barrier((acts[last], outs[last - 1]))
-    outs.append(down_product(acts[last], downs))
+        return placed.astype(jnp.bfloat16).reshape(experts, count * tall, lanes)
+
+    def halves(incoming, count):
+        middle = experts // 2
+        parts = (incoming[:middle], incoming[middle:])
+        return tuple(part.reshape(middle * count, width) for part in parts)
+
+    def dispatch(outgoing):
+        return lax.all_to_all(outgoing, "expert", split_axis=0, concat_axis=0, tiled=True)
+
+    outgoing, down_parts = lax.optimization_barrier(
+        (outgoing_rows(CHUNKS[0], places[0]), down_parts)
+    )
+    downs = tuple(shift(part, by) if by else part for part, by in zip(down_parts, (0, 1, -1, 2)))
+    own = halves(dispatch(outgoing), CHUNKS[0])
+    next_outgoing = outgoing_rows(CHUNKS[1], places[1])
+    next_outgoing, own = lax.optimization_barrier((next_outgoing, own))
+    next_outgoing, downs = lax.optimization_barrier((next_outgoing, downs))
+    next_arrived = dispatch(next_outgoing)
+    first = gather_neighbours(own)
+    next_arrived, _, _ = lax.optimization_barrier((next_arrived, first[0], first[3]))
+    second = (shift(first[0], 1), shift(first[3], -1))
+    late_sketch, next_arrived = lax.optimization_barrier((sketch, next_arrived))
+    full_sketch = lax.all_gather(late_sketch, "expert", axis=0, tiled=True)
+    next_own = halves(next_arrived, CHUNKS[1])
+    next_first = list(gather_neighbours(next_own))
+    second, _, _ = lax.optimization_barrier(
+        (second, next_first[0], next_first[3])
+    )
+    next_second = (shift(next_first[0], 1), shift(next_first[3], -1))
+    act = hidden_units((*own, *first, *second), w_gate, w_up)
+    acts = (act, shift(act, 1), shift(act, -1), shift(act, 2))
+    next_second, act = lax.optimization_barrier((next_second, act))
+    next_act = hidden_units((*next_own, *next_first, *next_second), w_gate, w_up)
+    next_acts = (next_act, shift(next_act, 1), shift(next_act, -1), shift(next_act, 2))
+    acts, next_act = lax.optimization_barrier((acts, next_act))
+    next_acts = (next_act, *next_acts[1:])
+    out = down_product(acts, downs)
+    next_acts, _ = lax.optimization_barrier((next_acts, out))
+    next_acts, full_sketch = lax.optimization_barrier((next_acts, full_sketch))
+    outs = (out, down_product(next_acts, downs))
 
     mixed_sum = jnp.zeros((groups, rows_dev, columns), jnp.float32)
     back = ()

time: 371 us -> 359 us (0.968)
  waiting for transfers between devices: 197 us -> 190 us
  local copies, waits for them, and re-layouts: 26.4 us -> 21.9 us
    all_to_all x2, waiting for transfers between devices: 61.9 us -> 32.7 us  [shards(): lax.all_to_all(out, ('dp', 'expert'), split_axis=0, concat_axis=0, tiled=...]
    ppermute x24, waiting for transfers between devices: 90.6 us -> 106 us  [shift(): return lax.ppermute(x, 'dp', [(i, (i + by) % size) for i in range(size)])]
    all_to_all x2, waiting for transfers between devices: 28 us -> 35.8 us  [dispatch(): lax.all_to_all(outgoing, 'expert', split_axis=0, concat_axis=0, tiled=True)]
    reshape x8 -> x6, local copies, waits for them, and re-layouts: 12.7 us -> 8.24 us  [the longest x2 4.43 us: outgoing_rows(): return placed.astype(jnp.bfloat16).reshape(experts, count * tall, lanes)]
  transfers between devices with their start and end apart: 31 -> 31, of which waited for: 16 -> 17; matrix products, arithmetic and copies ran while one was open for 5% -> 4% of each run, Pallas kernels for 9% -> 9%
where the time goes in v3:
time: 359 us; the launch traced here: 358 us
  waiting for transfers between devices  190 us (53%)
  starting transfers between devices  85.4 us (24%)
  Pallas kernels  32.1 us (9%)
  local copies, waits for them, and re-layouts  21.9 us (6%)
  between operations  14.4 us (4%)
  matrix products  10.8 us (3%)
    ppermute x24, waiting for transfers between devices, shift(): return lax.ppermute(x, 'dp', [(i, (i + by) % size) for i in range(size)])  106 us
    all_to_all x2, waiting for transfers between devices, dispatch(): lax.all_to_all(outgoing, 'expert', split_axis=0, concat_axis=0, tiled=True)  35.8 us
    all_to_all x2, waiting for transfers between devices, shards(): lax.all_to_all(out, ('dp', 'expert'), split_axis=0, concat_axis=0, tiled=...  32.7 us
    ppermute x24, starting transfers between devices, shift(): return lax.ppermute(x, 'dp', [(i, (i + by) % size) for i in range(size)])  29 us
    all_to_all x2, starting transfers between devices, shards(): lax.all_to_all(out, ('dp', 'expert'), split_axis=0, concat_axis=0, tiled=...  28.7 us
    all_to_all x2, starting transfers between devices, dispatch(): lax.all_to_all(outgoing, 'expert', split_axis=0, concat_axis=0, tiled=True)  19.3 us
    pallas_call x2, Pallas kernels, hidden_units(): pl.pallas_call(lambda *refs: hidden_kernel(steps, *refs), grid_spec=pltpu...  19.3 us
    all_to_all x1, waiting for transfers between devices, shards(): lax.all_to_all(parts, 'expert', split_axis=0, concat_axis=0, tiled=True)  16 us
  transfers between devices with their start and end apart: 31, of which 17 were waited for; matrix products, arithmetic and copies ran while one was open for 4% of the time, Pallas kernels for 9%

profile of v3, /device:TPU:1, one launch (start us, length us, event | category | flops | bytes accessed | tf_op | source)
XLA Modules:
  0.0 358.2 jit_solution(6605637096198305915)
XLA Ops:
  9.5 2.1 reshape.75
  11.6 3.6 %dynamic-slice_bitcast_fusion = (bf16[384,1024]{1,0:T(8,128)(2,1)}, bf16[384,1024]{1,0:T(8,128)(2,1)}, bf16[384,1024]{1,0:T(8,128)(2,1)}, bf16[384,1024]{1,0:T(8,128)(2,1)}) fusion(bf16[1,384,4096]{2,1,0:T(8,128)(2,1)} %param.14, s32[]{:T(128)S(6)} %select_n.140, s32[]{:T(128)S(6)} %select_n.138, s32[]{:T(128)S(6)} %select_n.137, s32[]{:T(128)S(6)} %select_n.139), kind=kLoop, calls=%fused_computation.10 | loop fusion | bytes 6291472 | tf_op jit(solution)/shard_map/dynamic_slice | solution.py:135
  15.2 13.2 %all-to-all-start = ((bf16[64,96,128]{2,1,0:T(8,128)(2,1)}), bf16[64,96,128]{2,1,0:T(8,128)(2,1)S(1)}, u32[]{:S(2)}, u32[]{:S(2)}) async-start(bf16[64,96,128]{2,1,0:T(8,128)(2,1)} %reshape.75), calls=%async_computation | async-start | bytes 3145728 | tf_op jit(solution)/shard_map/all_to_all | solution.py:150
  29.7 1.5 collective-permute-start.7
  31.1 1.5 collective-permute-start.8
  32.7 1.4 convolution_convert_fusion.1
  34.1 2.3 reshape.74
  36.4 31.7 %all-to-all-done = bf16[64,96,128]{2,1,0:T(8,128)(2,1)S(1)} async-done(((bf16[64,96,128]{2,1,0:T(8,128)(2,1)}), bf16[64,96,128]{2,1,0:T(8,128)(2,1)S(1)}, u32[]{:S(2)}, u32[]{:S(2)}) %all-to-all-start) | async-done | bytes 1572896 | tf_op jit(solution)/shard_map/all_to_all | solution.py:150
  69.1 2.1 reshape.76.refs_1_
  72.5 6.1 %all-to-all-start.1 = ((bf16[64,64,128]{2,1,0:T(8,128)(2,1)}), bf16[64,64,128]{2,1,0:T(8,128)(2,1)S(1)}, u32[]{:S(2)}, u32[]{:S(2)}) async-start(bf16[64,64,128]{2,1,0:T(8,128)(2,1)} %reshape.74), calls=%async_computation.1 | async-start | bytes 2097152 | tf_op jit(solution)/shard_map/all_to_all | solution.py:150
  80.0 1.5 collective-permute-start.3
  81.5 17.5 %collective-permute-done.refs_3_ = bf16[96,4096]{1,0:T(8,128)(2,1)} collective-permute-done((bf16[96,4096]{1,0:T(8,128)(2,1)}, bf16[96,4096]{1,0:T(8,128)(2,1)}, u32[]{:S(2)}, u32[]{:S(2)}) %collective-permute-start) | collective-permute-done | bytes 786464 | tf_op jit(solution)/shard_map/ppermute | solution.py:16
  100.2 1.5 collective-permute-start.2
  101.7 1.4 collective-permute-start.5
  103.1 4.1 %all-to-all-done.1 = bf16[64,64,128]{2,1,0:T(8,128)(2,1)S(1)} async-done(((bf16[64,64,128]{2,1,0:T(8,128)(2,1)}), bf16[64,64,128]{2,1,0:T(8,128)(2,1)S(1)}, u32[]{:S(2)}, u32[]{:S(2)}) %all-to-all-start.1) | async-done | bytes 1048608 | tf_op jit(solution)/shard_map/all_to_all | solution.py:150
  109.1 9.2 %collective-permute-done.4.refs_7_ = bf16[96,4096]{1,0:T(8,128)(2,1)} collective-permute-done((bf16[96,4096]{1,0:T(8,128)(2,1)}, bf16[96,4096]{1,0:T(8,128)(2,1)}, u32[]{:S(2)}, u32[]{:S(2)}) %collective-permute-start.4) | collective-permute-done | bytes 786464 | tf_op jit(solution)/shard_map/ppermute | solution.py:16
  118.3 27.9 %collective-permute-done.9.refs_3_ = bf16[64,4096]{1,0:T(8,128)(2,1)S(1)} collective-permute-done((bf16[64,4096]{1,0:T(8,128)(2,1)S(1)}, bf16[64,4096]{1,0:T(8,128)(2,1)S(1)}, u32[]{:S(2)}, u32[]{:S(2)}) %collective-permute-start.9) | collective-permute-done | bytes 524320 | tf_op jit(solution)/shard_map/ppermute | solution.py:16
  146.2 2.7 collective-permute-start.17
  149.0 2.7 collective-permute-start.15
  151.7 10.7 %shard_map.95.refs_0_ = bf16[768,384]{1,0:T(8,128)(2,1)} custom-call(s32[1]{0:T(128)} %bitcast.refs_0_, bf16[96,4096]{1,0:T(8,128)(2,1)} %reshape.76.refs_1_, bf16[96,4096]{1,0:T(8,128)(2,1)} %reshape.77.refs_2_, bf16[96,4096]{1,0:T(8,128)(2,1)} %collective-permute-done.refs_3_, bf16[96,4096]{1,0:T(8,128)(2,1)} %collective-permute-done.1.refs_4_, ...), custom_call_target="tpu_custom_call" | custom-call | flops 4831838208 | bytes 12582912 | tf_op jit(solution)/shard_map/pallas_call | solution.py:64
  162.5 2.7 collective-permute-start.12
  165.2 4.7 %collective-permute-done.14.refs_4_ = bf16[64,4096]{1,0:T(8,128)(2,1)S(1)} collective-permute-done((bf16[64,4096]{1,0:T(8,128)(2,1)S(1)}, bf16[64,4096]{1,0:T(8,128)(2,1)S(1)}, u32[]{:S(2)}, u32[]{:S(2)}) %collective-permute-start.14) | collective-permute-done | bytes 524320 | tf_op jit(solution)/shard_map/ppermute | solution.py:16
  171.4 8.6 %shard_map.96.refs_0_ = bf16[512,384]{1,0:T(8,128)(2,1)} custom-call(s32[1]{0:T(128)} %bitcast.refs_0_, bf16[64,4096]{1,0:T(8,128)(2,1)} %copy-done.3, bf16[64,4096]{1,0:T(8,128)(2,1)} %copy-done.2, bf16[64,4096]{1,0:T(8,128)(2,1)} %copy-done.8, bf16[64,4096]{1,0:T(8,128)(2,1)} %copy-done.9, bf16[64,4096]{1,0:T(8,128)(2,1)} %copy-done.10, ...), custom_call_target="tpu_custom_call" | custom-call | flops 3221225472 | bytes 10485760 | tf_op jit(solution)/shard_map/pallas_call | solution.py:64
  180.0 3.7 %collective-permute-done.11.refs_1_ = bf16[768,384]{1,0:T(8,128)(2,1)S(1)} collective-permute-done((bf16[768,384]{1,0:T(8,128)(2,1)}, bf16[768,384]{1,0:T(8,128)(2,1)S(1)}, u32[]{:S(2)}, u32[]{:S(2)}) %collective-permute-start.11) | collective-permute-done | bytes 589856 | tf_op jit(solution)/shard_map/ppermute | solution.py:16
  183.7 10.2 %collective-permute-done.13.refs_3_ = bf16[768,384]{1,0:T(8,128)(2,1)S(1)} collective-permute-done((bf16[768,384]{1,0:T(8,128)(2,1)}, bf16[768,384]{1,0:T(8,128)(2,1)S(1)}, u32[]{:S(2)}, u32[]{:S(2)}) %collective-permute-start.13) | collective-permute-done | bytes 589856 | tf_op jit(solution)/shard_map/ppermute | solution.py:16
  194.8 7.1 %shard_map.97 = bf16[768,8,128]{2,1,0:T(8,128)(2,1)} custom-call(bf16[768,384]{1,0:T(8,128)(2,1)} %shard_map.95.refs_0_, bf16[768,384]{1,0:T(8,128)(2,1)} %copy-done.5, bf16[768,384]{1,0:T(8,128)(2,1)} %copy-done.6, bf16[768,384]{1,0:T(8,128)(2,1)} %copy-done.7, bf16[384,1024]{1,0:T(8,128)(2,1)} %get-tuple-element.56.refs_4_, ...), custom_call_target="tpu_custom_call" | custom-call | flops 2415919104 | bytes 7077888 | tf_op jit(solution)/shard_map/pallas_call | solution.py:97
  202.0 17.9 %all-to-all-start.2 = ((bf16[256,24,128]{2,1,0:T(8,128)(2,1)}), bf16[256,24,128]{2,1,0:T(8,128)(2,1)S(1)}, u32[]{:S(2)}, u32[]{:S(2)}) async-start(bf16[256,24,128]{2,1,0:T(8,128)(2,1)} %bitcast.46), calls=%async_computation.2 | async-start | bytes 3145728 | tf_op jit(solution)/shard_map/all_to_all | solution.py:189
  219.9 1.5 collective-permute-start.18
  221.4 1.3 collective-permute-start.19
  222.7 1.7 collective-permute-start.20
  224.4 11.6 %collective-permute-done.18.refs_1_ = bf16[512,384]{1,0:T(8,128)(2,1)S(1)} collective-permute-done((bf16[512,384]{1,0:T(8,128)(2,1)S(1)}, bf16[512,384]{1,0:T(8,128)(2,1)S(1)}, u32[]{:S(2)}, u32[]{:S(2)}) %collective-permute-start.18) | collective-permute-done | bytes 393248 | tf_op jit(solution)/shard_map/ppermute | solution.py:16
  237.7 15.5 %collective-permute-done.20.refs_3_ = bf16[512,384]{1,0:T(8,128)(2,1)} collective-permute-done((bf16[512,384]{1,0:T(8,128)(2,1)S(1)}, bf16[512,384]{1,0:T(8,128)(2,1)}, u32[]{:S(2)}, u32[]{:S(2)}) %collective-permute-start.20) | collective-permute-done | bytes 393248 | tf_op jit(solution)/shard_map/ppermute | solution.py:16
  253.1 5.7 %shard_map.98 = bf16[512,8,128]{2,1,0:T(8,128)(2,1)} custom-call(bf16[512,384]{1,0:T(8,128)(2,1)} %shard_map.96.refs_0_, bf16[512,384]{1,0:T(8,128)(2,1)} %copy-done.12, bf16[512,384]{1,0:T(8,128)(2,1)} %copy-done.13, bf16[512,384]{1,0:T(8,128)(2,1)} %collective-permute-done.20.refs_3_, bf16[384,1024]{1,0:T(8,128)(2,1)} %get-tuple-element.56.refs_4_, ...), custom_call_target="tpu_custom_call" | custom-call | flops 1610612736 | bytes 5767168 | tf_op jit(solution)/shard_map/pallas_call | solution.py:97
  258.9 5.0 %all-to-all-done.2 = bf16[256,24,128]{2,1,0:T(8,128)(2,1)S(1)} async-done(((bf16[256,24,128]{2,1,0:T(8,128)(2,1)}), bf16[256,24,128]{2,1,0:T(8,128)(2,1)S(1)}, u32[]{:S(2)}, u32[]{:S(2)}) %all-to-all-start.2) | async-done | bytes 1572896 | tf_op jit(solution)/shard_map/all_to_all | solution.py:189
  263.8 2.1 reshape.81
  265.9 10.8 %all-to-all-start.3 = ((bf16[256,16,128]{2,1,0:T(8,128)(2,1)}), bf16[256,16,128]{2,1,0:T(8,128)(2,1)}, u32[]{:S(2)}, u32[]{:S(2)}) async-start(bf16[256,16,128]{2,1,0:T(8,128)(2,1)} %bitcast.47), calls=%async_computation.3 | async-start | bytes 2097152 | tf_op jit(solution)/shard_map/all_to_all | solution.py:189
  278.5 2.1 fusion.16
  280.6 27.7 %all-to-all-done.3 = bf16[256,16,128]{2,1,0:T(8,128)(2,1)} async-done(((bf16[256,16,128]{2,1,0:T(8,128)(2,1)}), bf16[256,16,128]{2,1,0:T(8,128)(2,1)}, u32[]{:S(2)}, u32[]{:S(2)}) %all-to-all-start.3) | async-done | bytes 1048608 | tf_op jit(solution)/shard_map/all_to_all | solution.py:189
  308.3 1.5 reshape.83
  309.8 2.1 add_convert_fusion
  311.9 1.3 fusion
  313.2 3.5 all-to-all-start.4
  316.7 2.2 fusion.1
  318.9 2.7 collective-permute-start.21
  322.8 2.6 collective-permute-done.21
  328.4 4.9 %all-to-all-start.5 = ((bf16[64,16,256]{2,1,0:T(8,128)(2,1)}), bf16[64,16,256]{2,1,0:T(8,128)(2,1)S(1)}, u32[]{:S(2)}, u32[]{:S(2)}) async-start(bf16[64,16,256]{2,1,0:T(8,128)(2,1)} %bitcast.17), calls=%async_computation.5 | async-start | bytes 1048576 | tf_op jit(solution)/shard_map/all_to_all | solution.py:233
  333.3 1.3 copy.33
  334.6 16.0 %all-to-all-done.5 = bf16[64,16,256]{2,1,0:T(8,128)(2,1)S(1)} async-done(((bf16[64,16,256]{2,1,0:T(8,128)(2,1)}), bf16[64,16,256]{2,1,0:T(8,128)(2,1)S(1)}, u32[]{:S(2)}, u32[]{:S(2)}) %all-to-all-start.5) | async-done | bytes 524320 | tf_op jit(solution)/shard_map/all_to_all | solution.py:233
  (82 shorter events, 21.2 us)
Async XLA Ops:
  7.2 1.7 copy-start
  15.2 53.0 %all-to-all-start = ((bf16[64,96,128]{2,1,0:T(8,128)(2,1)}), bf16[64,96,128]{2,1,0:T(8,128)(2,1)S(1)}, u32[]{:S(2)}, u32[]{:S(2)}) async-start(bf16[64,96,128]{2,1,0:T(8,128)(2,1)} %reshape.75), calls=%async_computation | async-start | bytes 3145728 | tf_op jit(solution)/shard_map/all_to_all | solution.py:150
  28.4 44.1 %collective-permute-start.6 = (bf16[384,1024]{1,0:T(8,128)(2,1)}, bf16[384,1024]{1,0:T(8,128)(2,1)}, u32[]{:S(2)}, u32[]{:S(2)}) collective-permute-start(bf16[384,1024]{1,0:T(8,128)(2,1)} %get-tuple-element.42), channel_id=1, source_target_pairs={{0,64},{64,128},{128,192},{192,0},{1,65},{65,129},{129,193},{193,1... | collective-permute-start | bytes 2359304 | tf_op jit(solution)/shard_map/ppermute | solution.py:16
  29.7 42.8 %collective-permute-start.7 = (bf16[384,1024]{1,0:T(8,128)(2,1)}, bf16[384,1024]{1,0:T(8,128)(2,1)}, u32[]{:S(2)}, u32[]{:S(2)}) collective-permute-start(bf16[384,1024]{1,0:T(8,128)(2,1)} %get-tuple-element.43), channel_id=1, source_target_pairs={{0,192},{64,0},{128,64},{192,128},{1,193},{65,1},{129,65},{193,129... | collective-permute-start | bytes 2359304 | tf_op jit(solution)/shard_map/ppermute | solution.py:16
  31.1 41.4 %collective-permute-start.8 = (bf16[384,1024]{1,0:T(8,128)(2,1)}, bf16[384,1024]{1,0:T(8,128)(2,1)}, u32[]{:S(2)}, u32[]{:S(2)}) collective-permute-start(bf16[384,1024]{1,0:T(8,128)(2,1)} %get-tuple-element.44), channel_id=1, source_target_pairs={{0,128},{64,192},{128,0},{192,64},{1,129},{65,193},{129,1},{193,65... | collective-permute-start | bytes 2359304 | tf_op jit(solution)/shard_map/ppermute | solution.py:16
  72.5 34.7 %all-to-all-start.1 = ((bf16[64,64,128]{2,1,0:T(8,128)(2,1)}), bf16[64,64,128]{2,1,0:T(8,128)(2,1)S(1)}, u32[]{:S(2)}, u32[]{:S(2)}) async-start(bf16[64,64,128]{2,1,0:T(8,128)(2,1)} %reshape.74), calls=%async_computation.1 | async-start | bytes 2097152 | tf_op jit(solution)/shard_map/all_to_all | solution.py:150
  78.7 174.5 %all-gather.2.cloned.1.call-start = ((), (), s32[]{:S(2)}) async-start(), calls=%async_computation.6 | async-start | bytes 2129920 | tf_op jit(solution)/shard_map/all_gather | solution.py:165
  78.7 20.3 %collective-permute-start = (bf16[96,4096]{1,0:T(8,128)(2,1)}, bf16[96,4096]{1,0:T(8,128)(2,1)}, u32[]{:S(2)}, u32[]{:S(2)}) collective-permute-start(bf16[96,4096]{1,0:T(8,128)(2,1)} %reshape.76.refs_1_), channel_id=1, source_target_pairs={{0,64},{64,128},{128,192},{192,0},{1,65},{65,129},{129,193},{193,1... | collective-permute-start | bytes 2359304 | tf_op jit(solution)/shard_map/ppermute | solution.py:16
  80.0 21.7 %collective-permute-start.3 = (bf16[96,4096]{1,0:T(8,128)(2,1)}, bf16[96,4096]{1,0:T(8,128)(2,1)}, u32[]{:S(2)}, u32[]{:S(2)}) collective-permute-start(bf16[96,4096]{1,0:T(8,128)(2,1)} %reshape.77.refs_2_), channel_id=1, source_target_pairs={{0,192},{64,0},{128,64},{192,128},{1,193},{65,1},{129,65},{193,129... | collective-permute-start | bytes 2359304 | tf_op jit(solution)/shard_map/ppermute | solution.py:16
  99.0 19.3 %collective-permute-start.4 = (bf16[96,4096]{1,0:T(8,128)(2,1)}, bf16[96,4096]{1,0:T(8,128)(2,1)}, u32[]{:S(2)}, u32[]{:S(2)}) collective-permute-start(bf16[96,4096]{1,0:T(8,128)(2,1)} %collective-permute-done.refs_3_), channel_id=1, source_target_pairs={{0,64},{64,128},{128,192},{192,0},{1,65},{65,129},{129,193},{193,1... | collective-permute-start | bytes 2359304 | tf_op jit(solution)/shard_map/ppermute | solution.py:16
  99.0 50.1 %collective-permute-start.1 = (bf16[96,4096]{1,0:T(8,128)(2,1)}, bf16[96,4096]{1,0:T(8,128)(2,1)}, u32[]{:S(2)}, u32[]{:S(2)}) collective-permute-start(bf16[96,4096]{1,0:T(8,128)(2,1)} %reshape.77.refs_2_), channel_id=1, source_target_pairs={{0,64},{64,128},{128,192},{192,0},{1,65},{65,129},{129,193},{193,1... | collective-permute-start | bytes 2359304 | tf_op jit(solution)/shard_map/ppermute | solution.py:16
  100.2 51.5 %collective-permute-start.2 = (bf16[96,4096]{1,0:T(8,128)(2,1)}, bf16[96,4096]{1,0:T(8,128)(2,1)}, u32[]{:S(2)}, u32[]{:S(2)}) collective-permute-start(bf16[96,4096]{1,0:T(8,128)(2,1)} %reshape.76.refs_1_), channel_id=1, source_target_pairs={{0,192},{64,0},{128,64},{192,128},{1,193},{65,1},{129,65},{193,129... | collective-permute-start | bytes 2359304 | tf_op jit(solution)/shard_map/ppermute | solution.py:16
  101.7 47.2 %collective-permute-start.5 = (bf16[96,4096]{1,0:T(8,128)(2,1)}, bf16[96,4096]{1,0:T(8,128)(2,1)}, u32[]{:S(2)}, u32[]{:S(2)}) collective-permute-start(bf16[96,4096]{1,0:T(8,128)(2,1)} %collective-permute-done.3.refs_6_), channel_id=1, source_target_pairs={{0,192},{64,0},{128,64},{192,128},{1,193},{65,1},{129,65},{193,129... | collective-permute-start | bytes 2359304 | tf_op jit(solution)/shard_map/ppermute | solution.py:16
  107.5 54.9 %copy-start.2 = (bf16[64,4096]{1,0:T(8,128)(2,1)}, bf16[64,4096]{1,0:T(8,128)(2,1)S(1)}, u32[]{:S(2)}) copy-start(bf16[64,4096]{1,0:T(8,128)(2,1)S(1)} %reshape.79.refs_2_) | copy-start | bytes 1572868
  107.8 54.7 %copy-start.3 = (bf16[64,4096]{1,0:T(8,128)(2,1)}, bf16[64,4096]{1,0:T(8,128)(2,1)S(1)}, u32[]{:S(2)}) copy-start(bf16[64,4096]{1,0:T(8,128)(2,1)S(1)} %reshape.78.refs_1_) | copy-start | bytes 1572868
  107.8 38.5 %collective-permute-start.9 = (bf16[64,4096]{1,0:T(8,128)(2,1)S(1)}, bf16[64,4096]{1,0:T(8,128)(2,1)S(1)}, u32[]{:S(2)}, u32[]{:S(2)}) collective-permute-start(bf16[64,4096]{1,0:T(8,128)(2,1)S(1)} %reshape.78.refs_1_), channel_id=1, source_target_pairs={{0,64},{64,128},{128,192},{192,0},{1,65},{65,129},{129,193},{193,1... | collective-permute-start | bytes 1572872 | tf_op jit(solution)/shard_map/ppermute | solution.py:16
  118.2 28.0 %collective-permute-start.10 = (bf16[64,4096]{1,0:T(8,128)(2,1)S(1)}, bf16[64,4096]{1,0:T(8,128)(2,1)}, u32[]{:S(2)}, u32[]{:S(2)}) collective-permute-start(bf16[64,4096]{1,0:T(8,128)(2,1)S(1)} %reshape.79.refs_2_), channel_id=1, source_target_pairs={{0,192},{64,0},{128,64},{192,128},{1,193},{65,1},{129,65},{193,129... | collective-permute-start | bytes 1572872 | tf_op jit(solution)/shard_map/ppermute | solution.py:16
  146.2 16.2 %copy-start.8 = (bf16[64,4096]{1,0:T(8,128)(2,1)}, bf16[64,4096]{1,0:T(8,128)(2,1)S(1)}, u32[]{:S(2)}) copy-start(bf16[64,4096]{1,0:T(8,128)(2,1)S(1)} %collective-permute-done.9.refs_3_) | copy-start | bytes 1572868
  146.2 16.3 %collective-permute-start.16 = (bf16[64,4096]{1,0:T(8,128)(2,1)S(1)}, bf16[64,4096]{1,0:T(8,128)(2,1)}, u32[]{:S(2)}, u32[]{:S(2)}) collective-permute-start(bf16[64,4096]{1,0:T(8,128)(2,1)S(1)} %collective-permute-done.9.refs_3_), channel_id=1, source_target_pairs={{0,64},{64,128},{128,192},{192,0},{1,65},{65,129},{129,193},{193,1... | collective-permute-start | bytes 1572872 | tf_op jit(solution)/shard_map/ppermute | solution.py:16
  146.2 19.0 %collective-permute-start.17 = (bf16[64,4096]{1,0:T(8,128)(2,1)}, bf16[64,4096]{1,0:T(8,128)(2,1)}, u32[]{:S(2)}, u32[]{:S(2)}) collective-permute-start(bf16[64,4096]{1,0:T(8,128)(2,1)} %collective-permute-done.10.refs_6_), channel_id=1, source_target_pairs={{0,192},{64,0},{128,64},{192,128},{1,193},{65,1},{129,65},{193,129... | collective-permute-start | bytes 1572872 | tf_op jit(solution)/shard_map/ppermute | solution.py:16
  148.9 20.9 %collective-permute-start.14 = (bf16[64,4096]{1,0:T(8,128)(2,1)S(1)}, bf16[64,4096]{1,0:T(8,128)(2,1)S(1)}, u32[]{:S(2)}, u32[]{:S(2)}) collective-permute-start(bf16[64,4096]{1,0:T(8,128)(2,1)S(1)} %reshape.79.refs_2_), channel_id=1, source_target_pairs={{0,64},{64,128},{128,192},{192,0},{1,65},{65,129},{129,193},{193,1... | collective-permute-start | bytes 1572872 | tf_op jit(solution)/shard_map/ppermute | solution.py:16
  149.0 20.8 %collective-permute-start.15 = (bf16[64,4096]{1,0:T(8,128)(2,1)S(1)}, bf16[64,4096]{1,0:T(8,128)(2,1)S(1)}, u32[]{:S(2)}, u32[]{:S(2)}) collective-permute-start(bf16[64,4096]{1,0:T(8,128)(2,1)S(1)} %reshape.78.refs_1_), channel_id=1, source_target_pairs={{0,192},{64,0},{128,64},{192,128},{1,193},{65,1},{129,65},{193,129... | collective-permute-start | bytes 1572872 | tf_op jit(solution)/shard_map/ppermute | solution.py:16
  162.4 21.3 %collective-permute-start.11 = (bf16[768,384]{1,0:T(8,128)(2,1)}, bf16[768,384]{1,0:T(8,128)(2,1)S(1)}, u32[]{:S(2)}, u32[]{:S(2)}) collective-permute-start(bf16[768,384]{1,0:T(8,128)(2,1)} %shard_map.95.refs_0_), channel_id=1, source_target_pairs={{0,64},{64,128},{128,192},{192,0},{1,65},{65,129},{129,193},{193,1... | collective-permute-start | bytes 1769480 | tf_op jit(solution)/shard_map/ppermute | solution.py:16
  162.5 21.2 %collective-permute-start.12 = (bf16[768,384]{1,0:T(8,128)(2,1)}, bf16[768,384]{1,0:T(8,128)(2,1)S(1)}, u32[]{:S(2)}, u32[]{:S(2)}) collective-permute-start(bf16[768,384]{1,0:T(8,128)(2,1)} %shard_map.95.refs_0_), channel_id=1, source_target_pairs={{0,192},{64,0},{128,64},{192,128},{1,193},{65,1},{129,65},{193,129... | collective-permute-start | bytes 1769480 | tf_op jit(solution)/shard_map/ppermute | solution.py:16
  165.2 28.8 %collective-permute-start.13 = (bf16[768,384]{1,0:T(8,128)(2,1)}, bf16[768,384]{1,0:T(8,128)(2,1)S(1)}, u32[]{:S(2)}, u32[]{:S(2)}) collective-permute-start(bf16[768,384]{1,0:T(8,128)(2,1)} %shard_map.95.refs_0_), channel_id=1, source_target_pairs={{0,128},{64,192},{128,0},{192,64},{1,129},{65,193},{129,1},{193,65... | collective-permute-start | bytes 1769480 | tf_op jit(solution)/shard_map/ppermute | solution.py:16
  169.9 0.8 copy-start.9
  170.7 0.8 copy-start.10
  183.7 10.2 %copy-start.5 = (bf16[768,384]{1,0:T(8,128)(2,1)}, bf16[768,384]{1,0:T(8,128)(2,1)S(1)}, u32[]{:S(2)}) copy-start(bf16[768,384]{1,0:T(8,128)(2,1)S(1)} %collective-permute-done.11.refs_1_) | copy-start | bytes 1769476
  183.7 10.2 %copy-start.6 = (bf16[768,384]{1,0:T(8,128)(2,1)}, bf16[768,384]{1,0:T(8,128)(2,1)S(1)}, u32[]{:S(2)}) copy-start(bf16[768,384]{1,0:T(8,128)(2,1)S(1)} %collective-permute-done.12.refs_2_) | copy-start | bytes 1769476
  194.0 0.9 copy-start.7
  202.0 18.0 %copy-start.11 = (bf16[512,384]{1,0:T(8,128)(2,1)S(1)}, bf16[512,384]{1,0:T(8,128)(2,1)}, u32[]{:S(2)}) copy-start(bf16[512,384]{1,0:T(8,128)(2,1)} %shard_map.96.refs_0_) | copy-start | bytes 1179652
  202.0 61.9 %all-to-all-start.2 = ((bf16[256,24,128]{2,1,0:T(8,128)(2,1)}), bf16[256,24,128]{2,1,0:T(8,128)(2,1)S(1)}, u32[]{:S(2)}, u32[]{:S(2)}) async-start(bf16[256,24,128]{2,1,0:T(8,128)(2,1)} %bitcast.46), calls=%async_computation.2 | async-start | bytes 3145728 | tf_op jit(solution)/shard_map/all_to_all | solution.py:189
  219.9 16.1 %collective-permute-start.18 = (bf16[512,384]{1,0:T(8,128)(2,1)S(1)}, bf16[512,384]{1,0:T(8,128)(2,1)S(1)}, u32[]{:S(2)}, u32[]{:S(2)}) collective-permute-start(bf16[512,384]{1,0:T(8,128)(2,1)S(1)} %copy-done.11), channel_id=1, source_target_pairs={{0,64},{64,128},{128,192},{192,0},{1,65},{65,129},{129,193},{193,1... | collective-permute-start | bytes 1179656 | tf_op jit(solution)/shard_map/ppermute | solution.py:16
  221.4 15.5 %collective-permute-start.19 = (bf16[512,384]{1,0:T(8,128)(2,1)S(1)}, bf16[512,384]{1,0:T(8,128)(2,1)S(1)}, u32[]{:S(2)}, u32[]{:S(2)}) collective-permute-start(bf16[512,384]{1,0:T(8,128)(2,1)S(1)} %copy-done.11), channel_id=1, source_target_pairs={{0,192},{64,0},{128,64},{192,128},{1,193},{65,1},{129,65},{193,129... | collective-permute-start | bytes 1179656 | tf_op jit(solution)/shard_map/ppermute | solution.py:16
  222.7 30.4 %collective-permute-start.20 = (bf16[512,384]{1,0:T(8,128)(2,1)S(1)}, bf16[512,384]{1,0:T(8,128)(2,1)}, u32[]{:S(2)}, u32[]{:S(2)}) collective-permute-start(bf16[512,384]{1,0:T(8,128)(2,1)S(1)} %copy-done.11), channel_id=1, source_target_pairs={{0,128},{64,192},{128,0},{192,64},{1,129},{65,193},{129,1},{193,65... | collective-permute-start | bytes 1179656 | tf_op jit(solution)/shard_map/ppermute | solution.py:16
  236.0 17.1 %copy-start.12 = (bf16[512,384]{1,0:T(8,128)(2,1)}, bf16[512,384]{1,0:T(8,128)(2,1)S(1)}, u32[]{:S(2)}) copy-start(bf16[512,384]{1,0:T(8,128)(2,1)S(1)} %collective-permute-done.18.refs_1_) | copy-start | bytes 1179652
  236.9 0.7 copy-start.13
  258.8 18.4 %copy-start.14 = (s32[1,128]{1,0:T(1,128)S(1)}, s32[1,128]{1,0:T(1,128)}, u32[]{:S(2)}) copy-start(s32[1,128]{1,0:T(1,128)} %param.11) | copy-start | bytes 1540
  258.8 19.5 %copy-start.4 = (bf16[128,2]{0,1:T(2,128)(2,1)S(1)}, bf16[128,2]{0,1:T(2,128)(2,1)}, u32[]{:S(2)}) copy-start(bf16[128,2]{0,1:T(2,128)(2,1)} %param.10) | copy-start | bytes 1540
  265.9 12.6 %copy-start.1 = (bf16[4,192,1024]{2,1,0:T(8,128)(2,1)S(1)}, bf16[4,192,1024]{2,1,0:T(8,128)(2,1)}, u32[]{:S(2)}) copy-start(bf16[4,192,1024]{2,1,0:T(8,128)(2,1)} %reshape.81) | copy-start | bytes 4718596
  265.9 42.4 %all-to-all-start.3 = ((bf16[256,16,128]{2,1,0:T(8,128)(2,1)}), bf16[256,16,128]{2,1,0:T(8,128)(2,1)}, u32[]{:S(2)}, u32[]{:S(2)}) async-start(bf16[256,16,128]{2,1,0:T(8,128)(2,1)} %bitcast.47), calls=%async_computation.3 | async-start | bytes 2097152 | tf_op jit(solution)/shard_map/all_to_all | solution.py:189
  313.2 14.0 %all-to-all-start.4 = ((bf16[4,64,1024]{2,1,0:T(8,128)(2,1)}), bf16[4,64,1024]{2,1,0:T(8,128)(2,1)S(1)}, u32[]{:S(2)}, u32[]{:S(2)}) async-start(bf16[4,64,1024]{2,1,0:T(8,128)(2,1)} %fusion), calls=%async_computation.4 | async-start | bytes 1048576 | tf_op jit(solution)/shard_map/all_to_all | solution.py:210
  318.9 6.4 %collective-permute-start.21 = (bf16[64,256]{1,0:T(8,128)(2,1)S(1)}, bf16[64,256]{1,0:T(8,128)(2,1)S(1)}, u32[]{:S(2)}, u32[]{:S(2)}) collective-permute-start(bf16[64,256]{1,0:T(8,128)(2,1)S(1)} %fusion.1), channel_id=1, source_target_pairs={{0,192},{64,0},{128,64},{192,128},{1,193},{65,1},{129,65},{193,129... | collective-permute-start | bytes 98312 | tf_op jit(solution)/shard_map/ppermute | solution.py:16
  321.6 4.8 %collective-permute-start.22 = (bf16[64,256]{1,0:T(8,128)(2,1)S(1)}, bf16[64,256]{1,0:T(8,128)(2,1)S(1)}, u32[]{:S(2)}, u32[]{:S(2)}) collective-permute-start(bf16[64,256]{1,0:T(8,128)(2,1)S(1)} %fusion.1), channel_id=1, source_target_pairs={{0,128},{64,192},{128,0},{192,64},{1,129},{65,193},{129,1},{193,65... | collective-permute-start | bytes 98312 | tf_op jit(solution)/shard_map/ppermute | solution.py:16
  322.2 5.0 %collective-permute-start.23 = (bf16[64,256]{1,0:T(8,128)(2,1)S(1)}, bf16[64,256]{1,0:T(8,128)(2,1)S(1)}, u32[]{:S(2)}, u32[]{:S(2)}) collective-permute-start(bf16[64,256]{1,0:T(8,128)(2,1)S(1)} %fusion.1), channel_id=1, source_target_pairs={{0,64},{64,128},{128,192},{192,0},{1,65},{65,129},{129,193},{193,1... | collective-permute-start | bytes 98312 | tf_op jit(solution)/shard_map/ppermute | solution.py:16
  328.4 22.2 %all-to-all-start.5 = ((bf16[64,16,256]{2,1,0:T(8,128)(2,1)}), bf16[64,16,256]{2,1,0:T(8,128)(2,1)S(1)}, u32[]{:S(2)}, u32[]{:S(2)}) async-start(bf16[64,16,256]{2,1,0:T(8,128)(2,1)} %bitcast.17), calls=%async_computation.5 | async-start | bytes 1048576 | tf_op jit(solution)/shard_map/all_to_all | solution.py:233
Sparse Core Ops, SparseCore 0:
  149.0 80.6 all-gather.1

commit v4 on v3

--- a/solution.py
+++ b/solution.py
@@ -149,9 +149,7 @@
     def dispatch(outgoing):
         return lax.all_to_all(outgoing, "expert", split_axis=0, concat_axis=0, tiled=True)
 
-    outgoing, down_parts = lax.optimization_barrier(
-        (outgoing_rows(CHUNKS[0], places[0]), down_parts)
-    )
+    outgoing = outgoing_rows(CHUNKS[0], places[0])
     downs = tuple(shift(part, by) if by else part for part, by in zip(down_parts, (0, 1, -1, 2)))
     own = halves(dispatch(outgoing), CHUNKS[0])
     next_outgoing = outgoing_rows(CHUNKS[1], places[1])
@@ -177,6 +175,7 @@
     acts, next_act = lax.optimization_barrier((acts, next_act))
     next_acts = (next_act, *next_acts[1:])
     out = down_product(acts, downs)
+    out, _ = lax.optimization_barrier((out, next_acts[1:3]))
     next_acts, _ = lax.optimization_barrier((next_acts, out))
     next_acts, full_sketch = lax.optimization_barrier((next_acts, full_sketch))
     outs = (out, down_product(next_acts, downs))

time: 359 us -> 355 us (0.989)
  waiting for transfers between devices: 190 us -> 186 us
    ppermute x24, waiting for transfers between devices: 106 us -> 91.3 us  [shift(): return lax.ppermute(x, 'dp', [(i, (i + by) % size) for i in range(size)])]
    all_to_all x2, waiting for transfers between devices: 32.7 us -> 46.5 us  [shards(): lax.all_to_all(out, ('dp', 'expert'), split_axis=0, concat_axis=0, tiled=...]
  transfers between devices with their start and end apart: 31 -> 31, of which waited for: 17 -> 16; matrix products, arithmetic and copies ran while one was open for 4% -> 5% of each run, Pallas kernels for 9% -> 9%
where the time goes in v4:
time: 355 us; the launch traced here: 354 us
  waiting for transfers between devices  186 us (52%)
  starting transfers between devices  85.7 us (24%)
  Pallas kernels  32.1 us (9%)
  local copies, waits for them, and re-layouts  21.9 us (6%)
  between operations  14.4 us (4%)
  matrix products  10.8 us (3%)
    ppermute x24, waiting for transfers between devices, shift(): return lax.ppermute(x, 'dp', [(i, (i + by) % size) for i in range(size)])  91.3 us
    all_to_all x2, waiting for transfers between devices, shards(): lax.all_to_all(out, ('dp', 'expert'), split_axis=0, concat_axis=0, tiled=...  46.5 us
    all_to_all x2, waiting for transfers between devices, dispatch(): lax.all_to_all(outgoing, 'expert', split_axis=0, concat_axis=0, tiled=True)  32.3 us
    ppermute x24, starting transfers between devices, shift(): return lax.ppermute(x, 'dp', [(i, (i + by) % size) for i in range(size)])  29.7 us
    all_to_all x2, starting transfers between devices, shards(): lax.all_to_all(out, ('dp', 'expert'), split_axis=0, concat_axis=0, tiled=...  25.7 us
    all_to_all x2, starting transfers between devices, dispatch(): lax.all_to_all(outgoing, 'expert', split_axis=0, concat_axis=0, tiled=True)  21.9 us
    pallas_call x2, Pallas kernels, hidden_units(): pl.pallas_call(lambda *refs: hidden_kernel(steps, *refs), grid_spec=pltpu...  19.2 us
    all_to_all x1, waiting for transfers between devices, shards(): lax.all_to_all(parts, 'expert', split_axis=0, concat_axis=0, tiled=True)  16 us
  transfers between devices with their start and end apart: 31, of which 16 were waited for; matrix products, arithmetic and copies ran while one was open for 5% of the time, Pallas kernels for 9%

profile of v4, /device:TPU:1, one launch (start us, length us, event | category | flops | bytes accessed | tf_op | source)
XLA Modules:
  0.0 354.3 jit_solution(11401223498350073768)
XLA Ops:
  9.5 2.2 reshape.75
  11.6 13.2 %all-to-all-start = ((bf16[64,96,128]{2,1,0:T(8,128)(2,1)}), bf16[64,96,128]{2,1,0:T(8,128)(2,1)S(1)}, u32[]{:S(2)}, u32[]{:S(2)}) async-start(bf16[64,96,128]{2,1,0:T(8,128)(2,1)} %reshape.75), calls=%async_computation | async-start | bytes 3145728 | tf_op jit(solution)/shard_map/all_to_all | solution.py:150
  24.8 3.6 %dynamic-slice_bitcast_fusion = (bf16[384,1024]{1,0:T(8,128)(2,1)}, bf16[384,1024]{1,0:T(8,128)(2,1)}, bf16[384,1024]{1,0:T(8,128)(2,1)}, bf16[384,1024]{1,0:T(8,128)(2,1)}) fusion(bf16[1,384,4096]{2,1,0:T(8,128)(2,1)} %param.14, s32[]{:T(128)S(6)} %select_n.140, s32[]{:T(128)S(6)} %select_n.138, s32[]{:T(128)S(6)} %select_n.137, s32[]{:T(128)S(6)} %select_n.139), kind=kLoop, calls=%fused_computation.10 | loop fusion | bytes 6291472 | tf_op jit(solution)/shard_map/dynamic_slice | solution.py:135
  29.6 1.5 collective-permute-start.7
  31.1 1.5 collective-permute-start.8
  32.6 1.4 convolution_convert_fusion.1
  34.0 2.3 reshape.74
  36.3 28.3 %all-to-all-done = bf16[64,96,128]{2,1,0:T(8,128)(2,1)S(1)} async-done(((bf16[64,96,128]{2,1,0:T(8,128)(2,1)}), bf16[64,96,128]{2,1,0:T(8,128)(2,1)S(1)}, u32[]{:S(2)}, u32[]{:S(2)}) %all-to-all-start) | async-done | bytes 1572896 | tf_op jit(solution)/shard_map/all_to_all | solution.py:150
  65.6 2.1 reshape.76.refs_1_
  67.7 1.2 reshape.77.refs_2_
  68.9 8.7 %all-to-all-start.1 = ((bf16[64,64,128]{2,1,0:T(8,128)(2,1)}), bf16[64,64,128]{2,1,0:T(8,128)(2,1)S(1)}, u32[]{:S(2)}, u32[]{:S(2)}) async-start(bf16[64,64,128]{2,1,0:T(8,128)(2,1)} %reshape.74), calls=%async_computation.1 | async-start | bytes 2097152 | tf_op jit(solution)/shard_map/all_to_all | solution.py:150
  78.7 1.8 collective-permute-start.3
  80.5 17.5 %collective-permute-done.refs_3_ = bf16[96,4096]{1,0:T(8,128)(2,1)} collective-permute-done((bf16[96,4096]{1,0:T(8,128)(2,1)}, bf16[96,4096]{1,0:T(8,128)(2,1)}, u32[]{:S(2)}, u32[]{:S(2)}) %collective-permute-start) | collective-permute-done | bytes 786464 | tf_op jit(solution)/shard_map/ppermute | solution.py:16
  98.0 2.7 collective-permute-start.2
  100.7 1.4 collective-permute-start.5
  102.1 4.1 %all-to-all-done.1 = bf16[64,64,128]{2,1,0:T(8,128)(2,1)S(1)} async-done(((bf16[64,64,128]{2,1,0:T(8,128)(2,1)}), bf16[64,64,128]{2,1,0:T(8,128)(2,1)S(1)}, u32[]{:S(2)}, u32[]{:S(2)}) %all-to-all-start.1) | async-done | bytes 1048608 | tf_op jit(solution)/shard_map/all_to_all | solution.py:150
  107.7 9.5 %collective-permute-done.4.refs_7_ = bf16[96,4096]{1,0:T(8,128)(2,1)} collective-permute-done((bf16[96,4096]{1,0:T(8,128)(2,1)}, bf16[96,4096]{1,0:T(8,128)(2,1)}, u32[]{:S(2)}, u32[]{:S(2)}) %collective-permute-start.4) | collective-permute-done | bytes 786464 | tf_op jit(solution)/shard_map/ppermute | solution.py:16
  117.3 28.0 %collective-permute-done.9.refs_3_ = bf16[64,4096]{1,0:T(8,128)(2,1)S(1)} collective-permute-done((bf16[64,4096]{1,0:T(8,128)(2,1)S(1)}, bf16[64,4096]{1,0:T(8,128)(2,1)S(1)}, u32[]{:S(2)}, u32[]{:S(2)}) %collective-permute-start.9) | collective-permute-done | bytes 524320 | tf_op jit(solution)/shard_map/ppermute | solution.py:16
  145.2 2.7 collective-permute-start.17
  148.1 2.7 collective-permute-start.15
  150.7 10.7 %shard_map.95.refs_0_ = bf16[768,384]{1,0:T(8,128)(2,1)} custom-call(s32[1]{0:T(128)} %bitcast.refs_0_, bf16[96,4096]{1,0:T(8,128)(2,1)} %reshape.76.refs_1_, bf16[96,4096]{1,0:T(8,128)(2,1)} %reshape.77.refs_2_, bf16[96,4096]{1,0:T(8,128)(2,1)} %collective-permute-done.refs_3_, bf16[96,4096]{1,0:T(8,128)(2,1)} %collective-permute-done.1.refs_4_, ...), custom_call_target="tpu_custom_call" | custom-call | flops 4831838208 | bytes 12582912 | tf_op jit(solution)/shard_map/pallas_call | solution.py:64
  161.6 2.7 collective-permute-start.12
  164.2 4.7 %collective-permute-done.14.refs_4_ = bf16[64,4096]{1,0:T(8,128)(2,1)S(1)} collective-permute-done((bf16[64,4096]{1,0:T(8,128)(2,1)S(1)}, bf16[64,4096]{1,0:T(8,128)(2,1)S(1)}, u32[]{:S(2)}, u32[]{:S(2)}) %collective-permute-start.14) | collective-permute-done | bytes 524320 | tf_op jit(solution)/shard_map/ppermute | solution.py:16
  170.5 8.5 %shard_map.96.refs_0_ = bf16[512,384]{1,0:T(8,128)(2,1)} custom-call(s32[1]{0:T(128)} %bitcast.refs_0_, bf16[64,4096]{1,0:T(8,128)(2,1)} %copy-done.3, bf16[64,4096]{1,0:T(8,128)(2,1)} %copy-done.2, bf16[64,4096]{1,0:T(8,128)(2,1)} %copy-done.8, bf16[64,4096]{1,0:T(8,128)(2,1)} %copy-done.9, bf16[64,4096]{1,0:T(8,128)(2,1)} %copy-done.10, ...), custom_call_target="tpu_custom_call" | custom-call | flops 3221225472 | bytes 10485760 | tf_op jit(solution)/shard_map/pallas_call | solution.py:64
  179.0 2.7 collective-permute-start.19
  181.7 1.8 collective-permute-done.11.refs_1_
  183.5 8.7 %collective-permute-done.13.refs_3_ = bf16[768,384]{1,0:T(8,128)(2,1)S(1)} collective-permute-done((bf16[768,384]{1,0:T(8,128)(2,1)}, bf16[768,384]{1,0:T(8,128)(2,1)S(1)}, u32[]{:S(2)}, u32[]{:S(2)}) %collective-permute-start.13) | collective-permute-done | bytes 589856 | tf_op jit(solution)/shard_map/ppermute | solution.py:16
  193.0 7.1 %shard_map.97 = bf16[768,8,128]{2,1,0:T(8,128)(2,1)} custom-call(bf16[768,384]{1,0:T(8,128)(2,1)} %shard_map.95.refs_0_, bf16[768,384]{1,0:T(8,128)(2,1)} %copy-done.5, bf16[768,384]{1,0:T(8,128)(2,1)} %copy-done.6, bf16[768,384]{1,0:T(8,128)(2,1)} %copy-done.7, bf16[384,1024]{1,0:T(8,128)(2,1)} %get-tuple-element.47.refs_4_, ...), custom_call_target="tpu_custom_call" | custom-call | flops 2415919104 | bytes 7077888 | tf_op jit(solution)/shard_map/pallas_call | solution.py:97
  200.1 2.6 collective-permute-done.18.refs_1_
  202.7 18.7 %all-to-all-start.2 = ((bf16[256,24,128]{2,1,0:T(8,128)(2,1)}), bf16[256,24,128]{2,1,0:T(8,128)(2,1)S(1)}, u32[]{:S(2)}, u32[]{:S(2)}) async-start(bf16[256,24,128]{2,1,0:T(8,128)(2,1)} %bitcast.46), calls=%async_computation.2 | async-start | bytes 3145728 | tf_op jit(solution)/shard_map/all_to_all | solution.py:188
  221.5 3.0 collective-permute-start.20
  224.4 14.1 %collective-permute-done.20.refs_3_ = bf16[512,384]{1,0:T(8,128)(2,1)S(1)} collective-permute-done((bf16[512,384]{1,0:T(8,128)(2,1)S(1)}, bf16[512,384]{1,0:T(8,128)(2,1)S(1)}, u32[]{:S(2)}, u32[]{:S(2)}) %collective-permute-start.20) | collective-permute-done | bytes 393248 | tf_op jit(solution)/shard_map/ppermute | solution.py:16
  239.3 5.7 %shard_map.98 = bf16[512,8,128]{2,1,0:T(8,128)(2,1)} custom-call(bf16[512,384]{1,0:T(8,128)(2,1)} %shard_map.96.refs_0_, bf16[512,384]{1,0:T(8,128)(2,1)} %collective-permute-done.18.refs_1_, bf16[512,384]{1,0:T(8,128)(2,1)} %collective-permute-done.19.refs_2_, bf16[512,384]{1,0:T(8,128)(2,1)} %copy-done.12, bf16[384,1024]{1,0:T(8,128)(2,1)} %get-tuple-element.47.refs_4_, ...), custom_call_target="tpu_custom_call" | custom-call | flops 1610612736 | bytes 5767168 | tf_op jit(solution)/shard_map/pallas_call | solution.py:97
  245.0 20.1 %all-to-all-done.2 = bf16[256,24,128]{2,1,0:T(8,128)(2,1)S(1)} async-done(((bf16[256,24,128]{2,1,0:T(8,128)(2,1)}), bf16[256,24,128]{2,1,0:T(8,128)(2,1)S(1)}, u32[]{:S(2)}, u32[]{:S(2)}) %all-to-all-start.2) | async-done | bytes 1572896 | tf_op jit(solution)/shard_map/all_to_all | solution.py:188
  265.1 2.1 reshape.81
  267.2 7.0 %all-to-all-start.3 = ((bf16[256,16,128]{2,1,0:T(8,128)(2,1)}), bf16[256,16,128]{2,1,0:T(8,128)(2,1)}, u32[]{:S(2)}, u32[]{:S(2)}) async-start(bf16[256,16,128]{2,1,0:T(8,128)(2,1)} %bitcast.47), calls=%async_computation.3 | async-start | bytes 2097152 | tf_op jit(solution)/shard_map/all_to_all | solution.py:188
  275.9 2.1 fusion.16
  277.9 26.4 %all-to-all-done.3 = bf16[256,16,128]{2,1,0:T(8,128)(2,1)} async-done(((bf16[256,16,128]{2,1,0:T(8,128)(2,1)}), bf16[256,16,128]{2,1,0:T(8,128)(2,1)}, u32[]{:S(2)}, u32[]{:S(2)}) %all-to-all-start.3) | async-done | bytes 1048608 | tf_op jit(solution)/shard_map/all_to_all | solution.py:188
  304.4 1.5 reshape.83
  305.9 2.1 add_convert_fusion
  308.0 1.3 fusion
  309.3 3.5 all-to-all-start.4
  312.8 2.2 fusion.1
  315.0 2.7 collective-permute-start.21
  318.9 2.6 collective-permute-done.21
  324.5 4.9 %all-to-all-start.5 = ((bf16[64,16,256]{2,1,0:T(8,128)(2,1)}), bf16[64,16,256]{2,1,0:T(8,128)(2,1)S(1)}, u32[]{:S(2)}, u32[]{:S(2)}) async-start(bf16[64,16,256]{2,1,0:T(8,128)(2,1)} %bitcast.17), calls=%async_computation.5 | async-start | bytes 1048576 | tf_op jit(solution)/shard_map/all_to_all | solution.py:232
  329.4 1.3 copy.33
  330.7 16.0 %all-to-all-done.5 = bf16[64,16,256]{2,1,0:T(8,128)(2,1)S(1)} async-done(((bf16[64,16,256]{2,1,0:T(8,128)(2,1)}), bf16[64,16,256]{2,1,0:T(8,128)(2,1)S(1)}, u32[]{:S(2)}, u32[]{:S(2)}) %all-to-all-start.5) | async-done | bytes 524320 | tf_op jit(solution)/shard_map/all_to_all | solution.py:232
  (80 shorter events, 16.9 us)
Async XLA Ops:
  7.2 1.7 copy-start
  11.6 53.0 %all-to-all-start = ((bf16[64,96,128]{2,1,0:T(8,128)(2,1)}), bf16[64,96,128]{2,1,0:T(8,128)(2,1)S(1)}, u32[]{:S(2)}, u32[]{:S(2)}) async-start(bf16[64,96,128]{2,1,0:T(8,128)(2,1)} %reshape.75), calls=%async_computation | async-start | bytes 3145728 | tf_op jit(solution)/shard_map/all_to_all | solution.py:150
  28.4 40.6 %collective-permute-start.6 = (bf16[384,1024]{1,0:T(8,128)(2,1)}, bf16[384,1024]{1,0:T(8,128)(2,1)}, u32[]{:S(2)}, u32[]{:S(2)}) collective-permute-start(bf16[384,1024]{1,0:T(8,128)(2,1)} %get-tuple-element.73), channel_id=1, source_target_pairs={{0,64},{64,128},{128,192},{192,0},{1,65},{65,129},{129,193},{193,1... | collective-permute-start | bytes 2359304 | tf_op jit(solution)/shard_map/ppermute | solution.py:16
  29.6 39.3 %collective-permute-start.7 = (bf16[384,1024]{1,0:T(8,128)(2,1)}, bf16[384,1024]{1,0:T(8,128)(2,1)}, u32[]{:S(2)}, u32[]{:S(2)}) collective-permute-start(bf16[384,1024]{1,0:T(8,128)(2,1)} %get-tuple-element.75), channel_id=1, source_target_pairs={{0,192},{64,0},{128,64},{192,128},{1,193},{65,1},{129,65},{193,129... | collective-permute-start | bytes 2359304 | tf_op jit(solution)/shard_map/ppermute | solution.py:16
  31.1 37.9 %collective-permute-start.8 = (bf16[384,1024]{1,0:T(8,128)(2,1)}, bf16[384,1024]{1,0:T(8,128)(2,1)}, u32[]{:S(2)}, u32[]{:S(2)}) collective-permute-start(bf16[384,1024]{1,0:T(8,128)(2,1)} %get-tuple-element.72), channel_id=1, source_target_pairs={{0,128},{64,192},{128,0},{192,64},{1,129},{65,193},{129,1},{193,65... | collective-permute-start | bytes 2359304 | tf_op jit(solution)/shard_map/ppermute | solution.py:16
  68.9 37.3 %all-to-all-start.1 = ((bf16[64,64,128]{2,1,0:T(8,128)(2,1)}), bf16[64,64,128]{2,1,0:T(8,128)(2,1)S(1)}, u32[]{:S(2)}, u32[]{:S(2)}) async-start(bf16[64,64,128]{2,1,0:T(8,128)(2,1)} %reshape.74), calls=%async_computation.1 | async-start | bytes 2097152 | tf_op jit(solution)/shard_map/all_to_all | solution.py:150
  77.7 160.9 %all-gather.2.cloned.1.call-start = ((), (), s32[]{:S(2)}) async-start(), calls=%async_computation.6 | async-start | bytes 2129920 | tf_op jit(solution)/shard_map/all_gather | solution.py:163
  77.7 20.3 %collective-permute-start = (bf16[96,4096]{1,0:T(8,128)(2,1)}, bf16[96,4096]{1,0:T(8,128)(2,1)}, u32[]{:S(2)}, u32[]{:S(2)}) collective-permute-start(bf16[96,4096]{1,0:T(8,128)(2,1)} %reshape.76.refs_1_), channel_id=1, source_target_pairs={{0,64},{64,128},{128,192},{192,0},{1,65},{65,129},{129,193},{193,1... | collective-permute-start | bytes 2359304 | tf_op jit(solution)/shard_map/ppermute | solution.py:16
  78.7 22.0 %collective-permute-start.3 = (bf16[96,4096]{1,0:T(8,128)(2,1)}, bf16[96,4096]{1,0:T(8,128)(2,1)}, u32[]{:S(2)}, u32[]{:S(2)}) collective-permute-start(bf16[96,4096]{1,0:T(8,128)(2,1)} %reshape.77.refs_2_), channel_id=1, source_target_pairs={{0,192},{64,0},{128,64},{192,128},{1,193},{65,1},{129,65},{193,129... | collective-permute-start | bytes 2359304 | tf_op jit(solution)/shard_map/ppermute | solution.py:16
  98.0 19.3 %collective-permute-start.4 = (bf16[96,4096]{1,0:T(8,128)(2,1)}, bf16[96,4096]{1,0:T(8,128)(2,1)}, u32[]{:S(2)}, u32[]{:S(2)}) collective-permute-start(bf16[96,4096]{1,0:T(8,128)(2,1)} %collective-permute-done.refs_3_), channel_id=1, source_target_pairs={{0,64},{64,128},{128,192},{192,0},{1,65},{65,129},{129,193},{193,1... | collective-permute-start | bytes 2359304 | tf_op jit(solution)/shard_map/ppermute | solution.py:16
  98.0 50.1 %collective-permute-start.1 = (bf16[96,4096]{1,0:T(8,128)(2,1)}, bf16[96,4096]{1,0:T(8,128)(2,1)}, u32[]{:S(2)}, u32[]{:S(2)}) collective-permute-start(bf16[96,4096]{1,0:T(8,128)(2,1)} %reshape.77.refs_2_), channel_id=1, source_target_pairs={{0,64},{64,128},{128,192},{192,0},{1,65},{65,129},{129,193},{193,1... | collective-permute-start | bytes 2359304 | tf_op jit(solution)/shard_map/ppermute | solution.py:16
  98.0 52.7 %collective-permute-start.2 = (bf16[96,4096]{1,0:T(8,128)(2,1)}, bf16[96,4096]{1,0:T(8,128)(2,1)}, u32[]{:S(2)}, u32[]{:S(2)}) collective-permute-start(bf16[96,4096]{1,0:T(8,128)(2,1)} %reshape.76.refs_1_), channel_id=1, source_target_pairs={{0,192},{64,0},{128,64},{192,128},{1,193},{65,1},{129,65},{193,129... | collective-permute-start | bytes 2359304 | tf_op jit(solution)/shard_map/ppermute | solution.py:16
  100.7 47.2 %collective-permute-start.5 = (bf16[96,4096]{1,0:T(8,128)(2,1)}, bf16[96,4096]{1,0:T(8,128)(2,1)}, u32[]{:S(2)}, u32[]{:S(2)}) collective-permute-start(bf16[96,4096]{1,0:T(8,128)(2,1)} %collective-permute-done.3.refs_6_), channel_id=1, source_target_pairs={{0,192},{64,0},{128,64},{192,128},{1,193},{65,1},{129,65},{193,129... | collective-permute-start | bytes 2359304 | tf_op jit(solution)/shard_map/ppermute | solution.py:16
  106.5 54.9 %copy-start.2 = (bf16[64,4096]{1,0:T(8,128)(2,1)}, bf16[64,4096]{1,0:T(8,128)(2,1)S(1)}, u32[]{:S(2)}) copy-start(bf16[64,4096]{1,0:T(8,128)(2,1)S(1)} %reshape.79.refs_2_) | copy-start | bytes 1572868
  106.8 54.7 %copy-start.3 = (bf16[64,4096]{1,0:T(8,128)(2,1)}, bf16[64,4096]{1,0:T(8,128)(2,1)S(1)}, u32[]{:S(2)}) copy-start(bf16[64,4096]{1,0:T(8,128)(2,1)S(1)} %reshape.78.refs_1_) | copy-start | bytes 1572868
  106.8 38.5 %collective-permute-start.9 = (bf16[64,4096]{1,0:T(8,128)(2,1)S(1)}, bf16[64,4096]{1,0:T(8,128)(2,1)S(1)}, u32[]{:S(2)}, u32[]{:S(2)}) collective-permute-start(bf16[64,4096]{1,0:T(8,128)(2,1)S(1)} %reshape.78.refs_1_), channel_id=1, source_target_pairs={{0,64},{64,128},{128,192},{192,0},{1,65},{65,129},{129,193},{193,1... | collective-permute-start | bytes 1572872 | tf_op jit(solution)/shard_map/ppermute | solution.py:16
  117.3 28.0 %collective-permute-start.10 = (bf16[64,4096]{1,0:T(8,128)(2,1)S(1)}, bf16[64,4096]{1,0:T(8,128)(2,1)}, u32[]{:S(2)}, u32[]{:S(2)}) collective-permute-start(bf16[64,4096]{1,0:T(8,128)(2,1)S(1)} %reshape.79.refs_2_), channel_id=1, source_target_pairs={{0,192},{64,0},{128,64},{192,128},{1,193},{65,1},{129,65},{193,129... | collective-permute-start | bytes 1572872 | tf_op jit(solution)/shard_map/ppermute | solution.py:16
  145.2 16.2 %copy-start.8 = (bf16[64,4096]{1,0:T(8,128)(2,1)}, bf16[64,4096]{1,0:T(8,128)(2,1)S(1)}, u32[]{:S(2)}) copy-start(bf16[64,4096]{1,0:T(8,128)(2,1)S(1)} %collective-permute-done.9.refs_3_) | copy-start | bytes 1572868
  145.2 16.3 %collective-permute-start.16 = (bf16[64,4096]{1,0:T(8,128)(2,1)S(1)}, bf16[64,4096]{1,0:T(8,128)(2,1)}, u32[]{:S(2)}, u32[]{:S(2)}) collective-permute-start(bf16[64,4096]{1,0:T(8,128)(2,1)S(1)} %collective-permute-done.9.refs_3_), channel_id=1, source_target_pairs={{0,64},{64,128},{128,192},{192,0},{1,65},{65,129},{129,193},{193,1... | collective-permute-start | bytes 1572872 | tf_op jit(solution)/shard_map/ppermute | solution.py:16
  145.2 19.0 %collective-permute-start.17 = (bf16[64,4096]{1,0:T(8,128)(2,1)}, bf16[64,4096]{1,0:T(8,128)(2,1)}, u32[]{:S(2)}, u32[]{:S(2)}) collective-permute-start(bf16[64,4096]{1,0:T(8,128)(2,1)} %collective-permute-done.10.refs_6_), channel_id=1, source_target_pairs={{0,192},{64,0},{128,64},{192,128},{1,193},{65,1},{129,65},{193,129... | collective-permute-start | bytes 1572872 | tf_op jit(solution)/shard_map/ppermute | solution.py:16
  148.0 20.9 %collective-permute-start.14 = (bf16[64,4096]{1,0:T(8,128)(2,1)S(1)}, bf16[64,4096]{1,0:T(8,128)(2,1)S(1)}, u32[]{:S(2)}, u32[]{:S(2)}) collective-permute-start(bf16[64,4096]{1,0:T(8,128)(2,1)S(1)} %reshape.79.refs_2_), channel_id=1, source_target_pairs={{0,64},{64,128},{128,192},{192,0},{1,65},{65,129},{129,193},{193,1... | collective-permute-start | bytes 1572872 | tf_op jit(solution)/shard_map/ppermute | solution.py:16
  148.1 20.8 %collective-permute-start.15 = (bf16[64,4096]{1,0:T(8,128)(2,1)S(1)}, bf16[64,4096]{1,0:T(8,128)(2,1)S(1)}, u32[]{:S(2)}, u32[]{:S(2)}) collective-permute-start(bf16[64,4096]{1,0:T(8,128)(2,1)S(1)} %reshape.78.refs_1_), channel_id=1, source_target_pairs={{0,192},{64,0},{128,64},{192,128},{1,193},{65,1},{129,65},{193,129... | collective-permute-start | bytes 1572872 | tf_op jit(solution)/shard_map/ppermute | solution.py:16
  161.5 22.1 %collective-permute-start.11 = (bf16[768,384]{1,0:T(8,128)(2,1)}, bf16[768,384]{1,0:T(8,128)(2,1)S(1)}, u32[]{:S(2)}, u32[]{:S(2)}) collective-permute-start(bf16[768,384]{1,0:T(8,128)(2,1)} %shard_map.95.refs_0_), channel_id=1, source_target_pairs={{0,64},{64,128},{128,192},{192,0},{1,65},{65,129},{129,193},{193,1... | collective-permute-start | bytes 1769480 | tf_op jit(solution)/shard_map/ppermute | solution.py:16
  161.6 22.0 %collective-permute-start.12 = (bf16[768,384]{1,0:T(8,128)(2,1)}, bf16[768,384]{1,0:T(8,128)(2,1)S(1)}, u32[]{:S(2)}, u32[]{:S(2)}) collective-permute-start(bf16[768,384]{1,0:T(8,128)(2,1)} %shard_map.95.refs_0_), channel_id=1, source_target_pairs={{0,192},{64,0},{128,64},{192,128},{1,193},{65,1},{129,65},{193,129... | collective-permute-start | bytes 1769480 | tf_op jit(solution)/shard_map/ppermute | solution.py:16
  164.2 28.0 %collective-permute-start.13 = (bf16[768,384]{1,0:T(8,128)(2,1)}, bf16[768,384]{1,0:T(8,128)(2,1)S(1)}, u32[]{:S(2)}, u32[]{:S(2)}) collective-permute-start(bf16[768,384]{1,0:T(8,128)(2,1)} %shard_map.95.refs_0_), channel_id=1, source_target_pairs={{0,128},{64,192},{128,0},{192,64},{1,129},{65,193},{129,1},{193,65... | collective-permute-start | bytes 1769480 | tf_op jit(solution)/shard_map/ppermute | solution.py:16
  168.9 0.8 copy-start.9
  169.7 0.8 copy-start.10
  179.0 23.7 %collective-permute-start.18 = (bf16[512,384]{1,0:T(8,128)(2,1)}, bf16[512,384]{1,0:T(8,128)(2,1)}, u32[]{:S(2)}, u32[]{:S(2)}) collective-permute-start(bf16[512,384]{1,0:T(8,128)(2,1)} %shard_map.96.refs_0_), channel_id=1, source_target_pairs={{0,64},{64,128},{128,192},{192,0},{1,65},{65,129},{129,193},{193,1... | collective-permute-start | bytes 1179656 | tf_op jit(solution)/shard_map/ppermute | solution.py:16
  179.0 23.7 %collective-permute-start.19 = (bf16[512,384]{1,0:T(8,128)(2,1)}, bf16[512,384]{1,0:T(8,128)(2,1)}, u32[]{:S(2)}, u32[]{:S(2)}) collective-permute-start(bf16[512,384]{1,0:T(8,128)(2,1)} %shard_map.96.refs_0_), channel_id=1, source_target_pairs={{0,192},{64,0},{128,64},{192,128},{1,193},{65,1},{129,65},{193,129... | collective-permute-start | bytes 1179656 | tf_op jit(solution)/shard_map/ppermute | solution.py:16
  183.5 8.7 %copy-start.5 = (bf16[768,384]{1,0:T(8,128)(2,1)}, bf16[768,384]{1,0:T(8,128)(2,1)S(1)}, u32[]{:S(2)}) copy-start(bf16[768,384]{1,0:T(8,128)(2,1)S(1)} %collective-permute-done.11.refs_1_) | copy-start | bytes 1769476
  183.5 8.7 %copy-start.6 = (bf16[768,384]{1,0:T(8,128)(2,1)}, bf16[768,384]{1,0:T(8,128)(2,1)S(1)}, u32[]{:S(2)}) copy-start(bf16[768,384]{1,0:T(8,128)(2,1)S(1)} %collective-permute-done.12.refs_2_) | copy-start | bytes 1769476
  192.2 0.8 copy-start.7
  200.1 21.3 %copy-start.11 = (bf16[512,384]{1,0:T(8,128)(2,1)S(1)}, bf16[512,384]{1,0:T(8,128)(2,1)}, u32[]{:S(2)}) copy-start(bf16[512,384]{1,0:T(8,128)(2,1)} %shard_map.96.refs_0_) | copy-start | bytes 1179652
  202.7 62.4 %all-to-all-start.2 = ((bf16[256,24,128]{2,1,0:T(8,128)(2,1)}), bf16[256,24,128]{2,1,0:T(8,128)(2,1)S(1)}, u32[]{:S(2)}, u32[]{:S(2)}) async-start(bf16[256,24,128]{2,1,0:T(8,128)(2,1)} %bitcast.46), calls=%async_computation.2 | async-start | bytes 3145728 | tf_op jit(solution)/shard_map/all_to_all | solution.py:188
  221.5 17.1 %collective-permute-start.20 = (bf16[512,384]{1,0:T(8,128)(2,1)S(1)}, bf16[512,384]{1,0:T(8,128)(2,1)S(1)}, u32[]{:S(2)}, u32[]{:S(2)}) collective-permute-start(bf16[512,384]{1,0:T(8,128)(2,1)S(1)} %copy-done.11), channel_id=1, source_target_pairs={{0,128},{64,192},{128,0},{192,64},{1,129},{65,193},{129,1},{193,65... | collective-permute-start | bytes 1179656 | tf_op jit(solution)/shard_map/ppermute | solution.py:16
  238.5 0.8 copy-start.12
  245.0 29.7 %copy-start.13 = (s32[1,128]{1,0:T(1,128)S(1)}, s32[1,128]{1,0:T(1,128)}, u32[]{:S(2)}) copy-start(s32[1,128]{1,0:T(1,128)} %param.11) | copy-start | bytes 1540
  245.0 30.7 %copy-start.4 = (bf16[128,2]{0,1:T(2,128)(2,1)S(1)}, bf16[128,2]{0,1:T(2,128)(2,1)}, u32[]{:S(2)}) copy-start(bf16[128,2]{0,1:T(2,128)(2,1)} %param.10) | copy-start | bytes 1540
  267.2 8.7 %copy-start.1 = (bf16[4,192,1024]{2,1,0:T(8,128)(2,1)S(1)}, bf16[4,192,1024]{2,1,0:T(8,128)(2,1)}, u32[]{:S(2)}) copy-start(bf16[4,192,1024]{2,1,0:T(8,128)(2,1)} %reshape.81) | copy-start | bytes 4718596
  267.2 37.2 %all-to-all-start.3 = ((bf16[256,16,128]{2,1,0:T(8,128)(2,1)}), bf16[256,16,128]{2,1,0:T(8,128)(2,1)}, u32[]{:S(2)}, u32[]{:S(2)}) async-start(bf16[256,16,128]{2,1,0:T(8,128)(2,1)} %bitcast.47), calls=%async_computation.3 | async-start | bytes 2097152 | tf_op jit(solution)/shard_map/all_to_all | solution.py:188
  309.3 14.0 %all-to-all-start.4 = ((bf16[4,64,1024]{2,1,0:T(8,128)(2,1)}), bf16[4,64,1024]{2,1,0:T(8,128)(2,1)S(1)}, u32[]{:S(2)}, u32[]{:S(2)}) async-start(bf16[4,64,1024]{2,1,0:T(8,128)(2,1)} %fusion), calls=%async_computation.4 | async-start | bytes 1048576 | tf_op jit(solution)/shard_map/all_to_all | solution.py:209
  315.0 6.4 %collective-permute-start.21 = (bf16[64,256]{1,0:T(8,128)(2,1)S(1)}, bf16[64,256]{1,0:T(8,128)(2,1)S(1)}, u32[]{:S(2)}, u32[]{:S(2)}) collective-permute-start(bf16[64,256]{1,0:T(8,128)(2,1)S(1)} %fusion.1), channel_id=1, source_target_pairs={{0,192},{64,0},{128,64},{192,128},{1,193},{65,1},{129,65},{193,129... | collective-permute-start | bytes 98312 | tf_op jit(solution)/shard_map/ppermute | solution.py:16
  317.7 4.8 %collective-permute-start.22 = (bf16[64,256]{1,0:T(8,128)(2,1)S(1)}, bf16[64,256]{1,0:T(8,128)(2,1)S(1)}, u32[]{:S(2)}, u32[]{:S(2)}) collective-permute-start(bf16[64,256]{1,0:T(8,128)(2,1)S(1)} %fusion.1), channel_id=1, source_target_pairs={{0,128},{64,192},{128,0},{192,64},{1,129},{65,193},{129,1},{193,65... | collective-permute-start | bytes 98312 | tf_op jit(solution)/shard_map/ppermute | solution.py:16
  318.3 5.0 %collective-permute-start.23 = (bf16[64,256]{1,0:T(8,128)(2,1)S(1)}, bf16[64,256]{1,0:T(8,128)(2,1)S(1)}, u32[]{:S(2)}, u32[]{:S(2)}) collective-permute-start(bf16[64,256]{1,0:T(8,128)(2,1)S(1)} %fusion.1), channel_id=1, source_target_pairs={{0,64},{64,128},{128,192},{192,0},{1,65},{65,129},{129,193},{193,1... | collective-permute-start | bytes 98312 | tf_op jit(solution)/shard_map/ppermute | solution.py:16
  324.5 22.2 %all-to-all-start.5 = ((bf16[64,16,256]{2,1,0:T(8,128)(2,1)}), bf16[64,16,256]{2,1,0:T(8,128)(2,1)S(1)}, u32[]{:S(2)}, u32[]{:S(2)}) async-start(bf16[64,16,256]{2,1,0:T(8,128)(2,1)} %bitcast.17), calls=%async_computation.5 | async-start | bytes 1048576 | tf_op jit(solution)/shard_map/all_to_all | solution.py:232
Sparse Core Ops, SparseCore 0:
  148.1 79.1 all-gather.1
